TPU v7x, 256 devices: a whole 4x4x8 slice. The times are simulated.
256 devices in a mesh: seq: 8 (over y, core), exp: 32 (over z, x).
Axes of the slice: x: 4, y: 4, z: 8, core: 2. Of those that a mesh axis runs over, the one named last changes fastest.
Arguments:
- queries: bfloat16 [2048, 64, 576], P('seq', 'exp')
- latent_cache: bfloat16 [32, 64, 576], P('seq')
- ancestors: int32 [32, 8], P('seq'), may hold values from -1 to 31, as said below
- value_up: bfloat16 [64, 512, 128], P('exp'), may hold values from -1 to 1
- out_proj: bfloat16 [8192, 7168], P('exp'), may hold values from -0.0625 to 0.0625
- residual: bfloat16 [2048, 7168], P(('seq', 'exp')), may hold values from -6 to 6
- norm_gain: bfloat16 [7168], replicated, may hold values from 0.099609375 to 1.8984375
- routes: int32 [2048, 8], P(('seq', 'exp')), may hold values from 0 to 31, all different within a row; in each aligned block of 8 rows (0 to 7, 8 to 15, ...) at most 3 rows name the same one
- gates: float32 [2048, 8], P(('seq', 'exp')), may hold values from 0.05 to 0.6
- w_gate: bfloat16 [32, 7168, 1024], P('exp', None, 'seq'), may hold values from -0.0625 to 0.0625
- w_up: bfloat16 [32, 7168, 1024], P('exp', None, 'seq'), may hold values from -0.0625 to 0.0625
- w_down: bfloat16 [32, 1024, 7168], P('exp', 'seq'), may hold values from -0.1875 to 0.1875
Outputs:
- layer_out: bfloat16 [2048, 7168], P(('seq', 'exp'))
Inputs may be any that keep to these rules, and one draw needn't show every extreme that they name: `ancestors`: each row lists distinct segments other than its own, listed ones first and then -1; every row lists at least one, some row lists 8 and some row exactly one. `routes`: within the 8 rows of one device no expert is named more than 3 times, a bound that some block reaches there.
All inputs are finite; a program needn't handle non-finite values.
Results may differ from a plain program's by a relative error of at most 0.024.
Values may be sent and summed in bfloat16 or wider, within the bound.
A program may use at most 128 MiB of HBM per device.

v0:
```python
import jax
import jax.numpy as jnp
from jax import lax
from jax.sharding import PartitionSpec as P

D = 7168
LAT = 512
ROPE = 64
HD = 128


neg_large = -1e30
eps_norm = 1e-06


def slot_positions(block_routes, experts, capacity):
    flat = block_routes.reshape(-1)
    onehot = (flat[:, None] == jnp.arange(experts, dtype=jnp.int32)[None, :]).astype(jnp.int32)
    before = jnp.cumsum(onehot, axis=0) - onehot
    slots = jnp.sum(before * onehot, axis=1)
    return (flat * capacity + slots).reshape(block_routes.shape)


def on_device(
    queries,
    latent_cache,
    ancestors,
    value_up,
    out_proj,
    residual,
    norm_gain,
    routes,
    gates,
    w_gate,
    w_up,
    w_down,
):
    tok_seq, head_dev, width = queries.shape
    seg_dev, block, _ = latent_cache.shape
    listed_count = ancestors.shape[1]
    tok_dev = residual.shape[0]
    scale = (HD + ROPE) ** (-0.5)
    query_blocks = queries.reshape(seg_dev, block, head_dev, width)
    gathered = lax.all_gather(latent_cache, "seq", axis=0, tiled=True)
    live = ancestors >= 0
    picked = gathered[jnp.maximum(ancestors, 0)].reshape(seg_dev, listed_count * block, width)
    keys = jnp.concatenate([picked, latent_cache], axis=1)
    causal = jnp.arange(block)[:, None] >= jnp.arange(block)[None, :]
    far_mask = jnp.broadcast_to(
        jnp.repeat(live, block, axis=1)[:, None, :], (seg_dev, block, listed_count * block)
    )
    near_mask = jnp.broadcast_to(causal[None, :, :], (seg_dev, block, block))
    mask = jnp.concatenate([far_mask, near_mask], axis=2)[:, :, None, :]
    scores = (
        jnp.einsum("sqhc,skc->sqhk", query_blocks, keys, preferred_element_type=jnp.float32) * scale
    )
    highest = jnp.max(jnp.where(mask, scores, neg_large), axis=-1, keepdims=True)
    weights = jnp.where(mask, jnp.exp(scores - highest), 0.0)
    total = jnp.sum(weights, axis=-1)
    summed = jnp.einsum(
        "sqhk,skc->sqhc",
        weights.astype(jnp.bfloat16),
        keys[:, :, :LAT],
        preferred_element_type=jnp.float32,
    )
    latent_out = (summed / total[..., None]).astype(jnp.bfloat16).reshape(tok_seq, head_dev, LAT)
    head_out = jnp.einsum("thc,hcv->thv", latent_out, value_up, preferred_element_type=jnp.float32)
    head_out = head_out.astype(jnp.bfloat16).reshape(tok_seq, head_dev * HD)
    rows = head_out
    attention = lax.psum_scatter(
        jnp.dot(rows, out_proj, preferred_element_type=jnp.float32).astype(jnp.bfloat16),
        "exp",
        scatter_dimension=0,
        tiled=True,
    ).astype(jnp.float32)
    hidden_state = residual.astype(jnp.float32) + attention
    inverse = lax.rsqrt(jnp.mean(hidden_state * hidden_state, axis=1, keepdims=True) + eps_norm)
    normed = (hidden_state * inverse * norm_gain.astype(jnp.float32)).astype(jnp.bfloat16)
    experts = lax.axis_size("exp")
    top = routes.shape[1]
    capacity = min(tok_dev, max(2, (tok_dev * top + experts - 1) // experts * 3 // 2))
    positions = slot_positions(routes, experts, capacity)
    selector = jnp.any(
        jnp.arange(experts * capacity, dtype=jnp.int32)[:, None, None] == positions[None, :, :],
        axis=2,
    )
    buffer = jnp.dot(selector.astype(jnp.bfloat16), normed, preferred_element_type=jnp.float32)
    buffer = buffer.astype(jnp.bfloat16).reshape(experts, capacity, D)
    gate_local = w_gate[0]
    up_local = w_up[0]
    down_local = w_down[0]
    arrived = lax.all_to_all(buffer, "exp", split_axis=0, concat_axis=0, tiled=True)
    piece = lax.all_gather(arrived, "seq", axis=0, tiled=True)
    shape = piece.shape
    rows = piece.reshape(-1, D)
    gate_val = jnp.dot(rows, gate_local, preferred_element_type=jnp.float32)
    up_val = jnp.dot(rows, up_local, preferred_element_type=jnp.float32)
    act = (jax.nn.silu(gate_val) * up_val).astype(jnp.bfloat16)
    partial_value = jnp.dot(act, down_local, preferred_element_type=jnp.float32).astype(
        jnp.bfloat16
    )
    partial_value = lax.optimization_barrier(partial_value).astype(jnp.float32)
    partial_value = partial_value.reshape(shape)
    summed_rows = lax.psum_scatter(
        partial_value.astype(jnp.bfloat16), "seq", scatter_dimension=0, tiled=True
    )
    returned = lax.all_to_all(summed_rows, "exp", split_axis=0, concat_axis=0, tiled=True).reshape(
        experts * capacity, D
    )
    combined = hidden_state
    for which in range(top):
        combined = combined + gates[:, which : which + 1] * returned[positions[:, which]].astype(
            jnp.float32
        )
    return combined.astype(jnp.bfloat16)


def solution(mesh):
    placed = (
        P("seq", "exp", None),
        P("seq", None, None),
        P("seq", None),
        P("exp", None, None),
        P("exp", None),
        P(("seq", "exp"), None),
        P(),
        P(("seq", "exp"), None),
        P(("seq", "exp"), None),
        P("exp", None, "seq"),
        P("exp", None, "seq"),
        P("exp", "seq", None),
    )
    return jax.shard_map(
        on_device, mesh=mesh, in_specs=placed, out_specs=P(("seq", "exp"), None), check_vma=False
    )
```

profile of v0, /device:TPU:32, one launch (start us, length us, event | category | flops | bytes accessed | tf_op | source)
XLA Modules:
  0.0 726.2 jit_solution(7309015356592234739)
XLA Ops:
  6.5 0.7 all-gather.3.cloned.1.call-update
  7.3 0.7 broadcast_maximum_fusion
  8.1 1.4 copy.25
  9.4 0.7 broadcast_compare_fusion
  10.4 30.1 %all-gather.3.cloned.1.call-done = bf16[32,64,576]{2,1,0:T(8,128)(2,1)} async-done(((bf16[4,64,576]{2,1,0:T(8,128)(2,1)}), bf16[32,64,576]{2,1,0:T(8,128)(2,1)}) %all-gather.3.cloned.1.call-update) | async-done | bytes 2359312 | tf_op jit(solution)/shard_map/all_gather | solution.py:44
  40.5 4.1 gather_fusion
  44.7 2.8 fusion.25
  47.5 0.6 fusion.64
  48.1 1.2 copy-done.3
  49.3 0.6 divide_convert_fusion
  49.9 0.3 copy-done.7
  50.2 0.3 convolution_convert_fusion.3
  50.5 0.9 copy-done.2
  51.4 2.9 convolution_convert_fusion.1
  54.4 0.6 copy-done.9
  55.7 219.1 %reduce-scatter.2.cloned.1.call-done = bf16[8,7168]{1,0:T(8,128)(2,1)} async-done(((bf16[256,7168]{1,0:T(8,128)(2,1)}), bf16[8,7168]{1,0:T(8,128)(2,1)}) %reduce-scatter.2.cloned.1.call-update) | async-done | bytes 114704 | tf_op jit(solution)/shard_map/reduce_scatter | solution.py:70
  274.8 1.1 multiply_reduce_fusion
  275.9 1.5 convolution_convert_fusion.2
  277.4 2.2 reshape.62
  279.6 47.7 %all_to_all.10 = bf16[32,3,7168]{2,1,0:T(4,128)(2,1)S(1)} all-to-all(bf16[32,3,7168]{2,1,0:T(4,128)(2,1)} %reshape.62), channel_id=1, replica_groups=mesh['seq'=8,'exp'=32] {'exp'}, dimensions={0} | all-to-all | bytes 2752512 | tf_op jit(solution)/shard_map/all_to_all | solution.py:92
  327.3 1.6 copy.29
  329.1 60.5 %all-gather.5.cloned.1.call-done = bf16[256,3,7168]{2,0,1:T(8,128)(2,1)} async-done(((bf16[32,3,7168]{2,0,1:T(8,128)(2,1)}), bf16[256,3,7168]{2,0,1:T(8,128)(2,1)}) %all-gather.5.cloned.1.call-update) | async-done | bytes 11010064 | tf_op jit(solution)/shard_map/all_gather | solution.py:93
  389.6 17.8 %copy.30 = bf16[256,3,7168]{2,1,0:T(4,128)(2,1)} copy(bf16[256,3,7168]{2,0,1:T(8,128)(2,1)} %all-gather.5.cloned.1.call-done) | data formatting | bytes 22020096 | tf_op jit(solution)/shard_map/all_gather | solution.py:93
  407.4 24.9 %reshape.63 = bf16[768,7168]{1,0:T(8,128)(2,1)} reshape(bf16[256,3,7168]{2,1,0:T(4,128)(2,1)} %copy.30) | data formatting | bytes 22020096 | tf_op jit(solution)/shard_map/reshape | solution.py:95
  432.4 6.3 fusion.12
  438.7 17.3 %convolution_convert_fusion = bf16[768,7168]{1,0:T(8,128)(2,1)} fusion(bf16[1,128,7168]{2,1,0:T(8,128)(2,1)S(1)} %copy-done, bf16[768,7168]{1,0:T(8,128)(2,1)} %reshape.63, bf16[1,7168,128]{2,1,0:T(8,128)(2,1)} %param.22, f32[768,128]{1,0:T(8,128)S(1)} %fusion.12), kind=kOutput, calls=%fused_computation.10 | convolution fusion | flops 2824667136 | bytes 26083328 | tf_op jit(solution)/shard_map/dot_general | solution.py:99
  456.0 23.4 %convert_element_type.85 = bf16[256,3,7168]{2,1,0:T(4,128)(2,1)} reshape(bf16[768,7168]{1,0:T(8,128)(2,1)} %convolution_convert_fusion) | data formatting | bytes 22020096 | tf_op jit(solution)/shard_map/convert_element_type | solution.py:105
  479.4 0.6 copy-done.11
  480.1 0.6 dynamic-slice
  481.3 167.3 %all-reduce.3.cloned.1.call-done = bf16[256,3,7168]{2,1,0:T(4,128)(2,1)} async-done(((bf16[256,3,7168]{2,1,0:T(4,128)(2,1)}), bf16[256,3,7168]{2,1,0:T(4,128)(2,1)}) %all-reduce.3.cloned.1.call-update) | async-done | bytes 11010064
  648.6 3.4 constant_dynamic-slice_fusion
  652.0 10.2 %all-to-all-start.1 = ((bf16[32,3,7168]{2,1,0:T(4,128)(2,1)}), bf16[32,3,7168]{2,1,0:T(4,128)(2,1)S(1)}, u32[]{:S(2)}, u32[]{:S(2)}) async-start(bf16[32,3,7168]{2,1,0:T(4,128)(2,1)} %constant_dynamic-slice_fusion), calls=%async_computation.2 | async-start | bytes 3670016 | tf_op jit(solution)/shard_map/all_to_all | solution.py:107
  662.2 0.3 fusion.52
  662.5 0.6 pad_clamp_fusion.4
  663.1 0.6 pad_clamp_fusion.2
  663.7 0.6 pad_clamp_fusion
  664.3 0.9 slice_reduce_fusion.7
  665.2 40.8 %all-to-all-done.1 = bf16[32,3,7168]{2,1,0:T(4,128)(2,1)S(1)} async-done(((bf16[32,3,7168]{2,1,0:T(4,128)(2,1)}), bf16[32,3,7168]{2,1,0:T(4,128)(2,1)S(1)}, u32[]{:S(2)}, u32[]{:S(2)}) %all-to-all-start.1) | async-done | bytes 1376288 | tf_op jit(solution)/shard_map/all_to_all | solution.py:107
  705.9 1.2 reshape.64
  707.1 0.6 gather_fusion.1
  707.8 1.3 gather_fusion.2
  709.0 1.3 gather_fusion.3
  710.3 1.5 gather_fusion.4
  711.8 1.5 gather_fusion.5
  713.3 1.4 gather_fusion.6
  714.7 1.4 gather_fusion.7
  716.1 1.4 gather_fusion.8
  717.5 2.2 add_convert_fusion
  (45 shorter events, 1.4 us)
Async XLA Ops:
  6.5 432.1 %copy-start = (bf16[1,128,7168]{2,1,0:T(8,128)(2,1)S(1)}, bf16[1,128,7168]{2,1,0:T(8,128)(2,1)}, u32[]{:S(2)}) copy-start(bf16[1,128,7168]{2,1,0:T(8,128)(2,1)} %param.23) | copy-start | bytes 5505028
  6.5 34.0 %all-gather.3.cloned.1.call-start = ((), (), s32[]{:S(2)}) async-start(), calls=%async_computation.3 | async-start | bytes 2949120 | tf_op jit(solution)/shard_map/all_gather | solution.py:44
  7.3 267.6 %reduce-scatter.2.cloned.1.call-start = ((), (), s32[]{:S(2)}) async-start(), calls=%async_computation.4 | async-start | bytes 3784704 | tf_op jit(solution)/shard_map/reduce_scatter | solution.py:70
  10.4 34.3 %copy-start.6 = (bf16[4,64,576]{2,1,0:T(8,128)(2,1)S(1)}, bf16[4,64,576]{2,1,0:T(8,128)(2,1)}, u32[]{:S(2)}) copy-start(bf16[4,64,576]{2,1,0:T(8,128)(2,1)} %param.13) | copy-start | bytes 884740
  47.5 1.7 copy-start.3
  49.3 0.9 copy-start.7
  49.3 2.1 copy-start.2
  54.3 0.7 copy-start.9
  54.3 1.2 copy-start.10
  54.3 220.5 %copy-start.4 = (bf16[8,7168]{1,0:T(8,128)(2,1)S(1)}, bf16[8,7168]{1,0:T(8,128)(2,1)}, u32[]{:S(2)}) copy-start(bf16[8,7168]{1,0:T(8,128)(2,1)} %param.17) | copy-start | bytes 344068
  54.4 335.3 %all-gather.5.cloned.1.call-start = ((), (), s32[]{:S(2)}) async-start(), calls=%async_computation.5 | async-start | bytes 12386304 | tf_op jit(solution)/shard_map/all_gather | solution.py:93
  328.9 319.7 %all-reduce.3.cloned.1.call-start = ((), (), s32[]{:S(2)}) async-start(), calls=%async_computation.6 | async-start | bytes 29360128
  479.4 0.7 copy-start.11
  652.0 12.3 %copy-start.8 = (f32[8,8]{1,0:T(8,128)S(1)}, f32[8,8]{1,0:T(8,128)}, u32[]{:S(2)}) copy-start(f32[8,8]{1,0:T(8,128)} %param.20) | copy-start | bytes 772
  652.0 53.9 %all-to-all-start.1 = ((bf16[32,3,7168]{2,1,0:T(4,128)(2,1)}), bf16[32,3,7168]{2,1,0:T(4,128)(2,1)S(1)}, u32[]{:S(2)}, u32[]{:S(2)}) async-start(bf16[32,3,7168]{2,1,0:T(4,128)(2,1)} %constant_dynamic-slice_fusion), calls=%async_computation.2 | async-start | bytes 3670016 | tf_op jit(solution)/shard_map/all_to_all | solution.py:107
  710.3 7.2 copy-start.5
  711.8 7.8 %copy-start.1 = (bf16[1,128,7168]{2,1,0:T(8,128)(2,1)S(1)}, bf16[1,128,7168]{2,1,0:T(8,128)(2,1)}, u32[]{:S(2)}) copy-start(bf16[1,128,7168]{2,1,0:T(8,128)(2,1)} %param.23) | copy-start | bytes 5505028
Sparse Core Ops, SparseCore 0:
  9.2 31.3 all-gather.2
  54.5 220.2 reduce-scatter.1
  329.0 60.5 all-gather.4
  479.6 168.9 all-reduce.2
where the time goes:
time: 730 us; the launch traced here: 726 us
  waiting for transfers between devices  519 us (71%)
  local copies, waits for them, and re-layouts  96 us (13%)
  blocking collectives  47.7 us (7%)
  matrix products  31.8 us (4%)
  between operations  14 us (2%)
  starting transfers between devices  10.5 us (1%)
  other arithmetic  7.75 us (1%)
    reduce_scatter x1, waiting for transfers between devices, on_device(): lax.psum_scatter(jnp.dot(rows, out_proj, preferred_element_type=jnp.float...  219 us
    unnamed x5, waiting for transfers between devices  168 us
    all_gather x1, waiting for transfers between devices, on_device(): piece = lax.all_gather(arrived, 'seq', axis=0, tiled=True)  60.5 us
    all_to_all x1, blocking collectives, on_device(): lax.all_to_all(buffer, 'exp', split_axis=0, concat_axis=0, tiled=True)  47.7 us
    all_to_all x1, waiting for transfers between devices, on_device(): lax.all_to_all(summed_rows, 'exp', split_axis=0, concat_axis=0, tiled=True)  40.8 us
    all_gather x1, waiting for transfers between devices, on_device(): gathered = lax.all_gather(latent_cache, 'seq', axis=0, tiled=True)  30.1 us
    reshape x1, local copies, waits for them, and re-layouts, on_device(): rows = piece.reshape(-1, D)  24.9 us
    convert_element_type x1, local copies, waits for them, and re-layouts, on_device(): partial_value.astype(jnp.bfloat16)  23.4 us
  transfers between devices with their start and end apart: 5, of which 5 were waited for; matrix products, arithmetic and copies ran while one was open for 1% of the time, Pallas kernels for 0%

commit v1 on v0

v1 whole, which is shorter than its diff:
```python
import jax
import jax.numpy as jnp
from jax import lax
from jax.experimental import pallas as pl
from jax.experimental.pallas import tpu as pltpu
from jax.sharding import PartitionSpec as P

D = 7168
LAT = 512
ROPE = 64
HD = 128
BLK = 64
ANC = 8
TOP = 8
EXPERTS = 32
CAP = 3
NY, NZ, NX = 4, 8, 4
DY = D // NY
CW = 512
FF = 1024
NORM_EPS = 1e-6
MASKED = -1e30
F32 = jnp.float32
BF16 = jnp.bfloat16
ANY = pl.BlockSpec(memory_space=pl.ANY)
VMEM = pl.BlockSpec(memory_space=pltpu.VMEM)
SMEM = pl.BlockSpec(memory_space=pltpu.SMEM)
DMA = pltpu.SemaphoreType.DMA


def place():
    s = lax.axis_index("seq")
    e = lax.axis_index("exp")
    return lax.div(s, 2), lax.rem(s, 2), lax.div(e, NX), lax.rem(e, NX)


def wrap(value, count):
    return lax.rem(value + count, count)


def remote(src, dst, send_sem, recv_sem, y, c, z, x):
    return pltpu.make_async_remote_copy(
        src_ref=src,
        dst_ref=dst,
        send_sem=send_sem,
        recv_sem=recv_sem,
        device_id=(y * 2 + c, z * NX + x),
        device_id_type=pl.DeviceIdType.MESH,
    )


def meet(peers):
    barrier = pltpu.get_barrier_semaphore()
    for y, c, z, x in peers:
        pl.semaphore_signal(
            barrier,
            inc=1,
            device_id=(y * 2 + c, z * NX + x),
            device_id_type=pl.DeviceIdType.MESH,
        )
    pl.semaphore_wait(barrier, len(peers))


def y_peers(y, c, z, x):
    return [(wrap(y + d, NY), c, z, x) for d in range(1, NY)]


def z_peers(y, c, z, x):
    return [(y, c, wrap(z + d, NZ), x) for d in range(1, NZ)]


def x_peers(y, c, z, x):
    return [(y, c, z, wrap(x + d, NX)) for d in range(1, NX)]


def column_start(x):
    return jnp.minimum(x * CW, DY - CW)


def pre_kernel(
    lat, outp, meta, res, lat_all, op_all, meta_all, res_y,
    loc, lat_s, lat_r, fwd_s, fwd_r, op_s, op_r, me_s, me_r, mz_s, mz_r, re_s, re_r,
):
    y, c, z, x = place()
    s = y * 2 + c
    other = 1 - c
    meet(
        y_peers(y, c, z, x) + z_peers(y, c, z, x) + x_peers(y, c, z, x) + [(y, other, z, x)]
    )
    started = []

    def go(copy):
        copy.start()
        started.append(copy)

    for d in range(1, NY):
        go(remote(lat, lat_all.at[s], lat_s.at[d], lat_r.at[d], wrap(y + d, NY), c, z, x))
    go(remote(lat, lat_all.at[s], fwd_s.at[0], fwd_r.at[0], y, other, z, x))

    def columns(to):
        start = pl.multiple_of(y * DY + column_start(to), 128)
        return outp.at[:, pl.ds(start, CW)]

    for d in range(1, NY):
        to = wrap(y + d, NY)
        go(remote(meta, meta_all.at[z, y], me_s.at[d], me_r.at[d], to, c, z, x))
        part = res.at[:, pl.ds(pl.multiple_of(to * DY, 128), DY)]
        go(remote(part, res_y.at[y], re_s.at[d], re_r.at[d], to, c, z, x))
    for d in range(1, NX):
        to = wrap(x + d, NX)
        go(remote(columns(to), op_all.at[x], op_s.at[d], op_r.at[d], y, c, z, to))
    own = [
        pltpu.make_async_copy(meta, meta_all.at[z, y], loc.at[0]),
        pltpu.make_async_copy(lat, lat_all.at[s], loc.at[1]),
        pltpu.make_async_copy(columns(x), op_all.at[x], loc.at[2]),
        pltpu.make_async_copy(
            res.at[:, pl.ds(pl.multiple_of(y * DY, 128), DY)], res_y.at[y], loc.at[3]
        ),
    ]
    for copy in own:
        copy.start()

    own[0].wait()
    for d in range(1, NY):
        src = wrap(y - d, NY)
        remote(meta, meta_all.at[z, src], me_s.at[d], me_r.at[d], y, c, z, x).wait_recv()
    for d in range(1, NZ):
        go(remote(meta_all.at[z], meta_all.at[z], mz_s.at[d], mz_r.at[d], y, c, wrap(z + d, NZ), x))
    for d in (1, 3, 2):
        block = lat_all.at[wrap(y - d, NY) * 2 + c]
        remote(lat, block, lat_s.at[d], lat_r.at[d], y, c, z, x).wait_recv()
        go(remote(block, block, fwd_s.at[d], fwd_r.at[d], y, other, z, x))
    for d in range(NY):
        block = lat_all.at[wrap(y - d, NY) * 2 + other]
        remote(lat, block, fwd_s.at[d], fwd_r.at[d], y, c, z, x).wait_recv()
    for d in range(1, NZ):
        src = meta_all.at[wrap(z - d, NZ)]
        remote(src, src, mz_s.at[d], mz_r.at[d], y, c, z, x).wait_recv()
    for d in range(1, NX):
        src = op_all.at[wrap(x - d, NX)]
        remote(src, src, op_s.at[d], op_r.at[d], y, c, z, x).wait_recv()
    for d in range(1, NY):
        src = res_y.at[wrap(y - d, NY)]
        remote(src, src, re_s.at[d], re_r.at[d], y, c, z, x).wait_recv()
    for copy in own[1:]:
        copy.wait()
    for copy in started:
        copy.wait_send()


def exchange_first(lat, outp, meta, res):
    return pl.pallas_call(
        pre_kernel,
        out_shape=(
            jax.ShapeDtypeStruct((8,) + lat.shape, BF16),
            jax.ShapeDtypeStruct((NX, 256, CW), BF16),
            jax.ShapeDtypeStruct((NZ, NY, 8, 128), F32),
            jax.ShapeDtypeStruct((NY, 8, DY), F32),
        ),
        in_specs=[ANY] * 4,
        out_specs=(ANY,) * 4,
        scratch_shapes=[
            DMA((4,)),
            DMA((NY,)), DMA((NY,)),
            DMA((NY,)), DMA((NY,)),
            DMA((NX,)), DMA((NX,)),
            DMA((NY,)), DMA((NY,)),
            DMA((NZ,)), DMA((NZ,)),
            DMA((NY,)), DMA((NY,)),
        ],
        compiler_params=pltpu.CompilerParams(collective_id=0, has_side_effects=True),
        name="exchange_first",
    )(lat, outp, meta, res)


def attend_kernel(anc, q, lat_all, live, vup, out, keys):
    s = lax.axis_index("seq")
    scale = (HD + ROPE) ** (-0.5)
    width = (ANC + 1) * BLK
    col = lax.broadcasted_iota(jnp.int32, (2 * BLK, width), 1)
    row = lax.rem(lax.broadcasted_iota(jnp.int32, (2 * BLK, width), 0), BLK)
    near = row >= col - ANC * BLK
    for g in range(4):
        for a in range(ANC):
            keys[a * BLK : (a + 1) * BLK, :] = lat_all[jnp.maximum(anc[g, a], 0)]
        keys[ANC * BLK :, :] = lat_all[s * 4 + g]
        query = q[:, g * BLK : (g + 1) * BLK, :].reshape(2 * BLK, LAT + ROPE)
        scores = (
            lax.dot_general(
                query, keys[...], (((1,), (1,)), ((), ())), preferred_element_type=F32
            )
            * scale
        )
        mask = jnp.logical_and(near, live[g : g + 1, :] > 0.5)
        highest = jnp.max(jnp.where(mask, scores, MASKED), axis=1, keepdims=True)
        weights = jnp.where(mask, jnp.exp(scores - highest), 0.0)
        total = jnp.sum(weights, axis=1, keepdims=True)
        summed = jnp.dot(weights.astype(BF16), keys[:, :LAT], preferred_element_type=F32)
        latent = (summed / total).astype(BF16)
        for h in range(2):
            value = jnp.dot(
                latent[h * BLK : (h + 1) * BLK], vup[h], preferred_element_type=F32
            )
            out[g * BLK : (g + 1) * BLK, h * HD : (h + 1) * HD] = value.astype(BF16)


def attend(anc, q, lat_all, live, vup):
    return pl.pallas_call(
        attend_kernel,
        out_shape=jax.ShapeDtypeStruct((256, 256), BF16),
        in_specs=[SMEM, VMEM, VMEM, VMEM, VMEM],
        out_specs=VMEM,
        scratch_shapes=[pltpu.VMEM(((ANC + 1) * BLK, LAT + ROPE), BF16)],
        compiler_params=pltpu.CompilerParams(vmem_limit_bytes=24 << 20),
        name="attend",
    )(anc, q, lat_all, live, vup)


def mid_kernel(
    ho, op_all, res_y, gain, choose, wg, wu, wd,
    hidden, rows, wg_all, wu_all, wd_all,
    ho_all, zsend, zrecv, att, xrecv, squares, tokens, disp,
    loc, ho_s, ho_r, zs, zr, xs, xr, qs, qr, ts, tr, ds, dr, w_s, w_r, f_s, f_r,
):
    y, c, z, x = place()
    s = y * 2 + c
    other = 1 - c
    corners = [
        (dy, dx) for dy in range(NY) for dx in range(NX) if (dy, dx) != (0, 0)
    ]
    meet(
        [(wrap(y + dy, NY), c, z, wrap(x + dx, NX)) for dy, dx in corners]
        + z_peers(y, c, z, x)
        + [(y, other, z, x)]
    )
    started = []

    def go(copy):
        copy.start()
        started.append(copy)

    for dy, dx in corners:
        i = dy * NX + dx
        go(
            remote(
                ho, ho_all.at[y, x], ho_s.at[i], ho_r.at[i],
                wrap(y + dy, NY), c, z, wrap(x + dx, NX),
            )
        )
    ho_all[y, x] = ho[...]

    def weight_parts(to):
        at = pl.ds(pl.multiple_of(to * DY, 128), DY)
        return (
            (wg.at[at, :], wg_all, 0),
            (wu.at[at, :], wu_all, 1),
            (wd.at[:, at], wd_all, 2),
        )

    own = []
    for src, dst, k in weight_parts(y):
        own.append(pltpu.make_async_copy(src, dst.at[s], loc.at[k]))
        go(remote(src, dst.at[s], f_s.at[k, 0], f_r.at[k, 0], y, other, z, x))
    for copy in own:
        copy.start()

    for dy in range(NY):
        ys = wrap(y - dy, NY)
        total = None
        for dx in range(NX):
            xn = wrap(x - dx, NX)
            i = dy * NX + dx
            if i:
                remote(ho, ho_all.at[ys, xn], ho_s.at[i], ho_r.at[i], y, c, z, x).wait_recv()
            part = jnp.dot(ho_all[ys, xn], op_all[xn], preferred_element_type=F32)
            total = part if total is None else total + part
        total = total.astype(BF16)
        for k in range(NZ):
            zsend[k, ys] = total[k * 32 : (k + 1) * 32]
        for d in range(1, NZ):
            to = wrap(z + d, NZ)
            go(
                remote(
                    zsend.at[to, ys], zrecv.at[d, ys], zs.at[d, dy], zr.at[d, dy], y, c, to, x
                )
            )
    for d in (1, 3, 2):
        to = wrap(y + d, NY)
        for src, dst, k in weight_parts(to):
            go(remote(src, dst.at[s], w_s.at[k, d], w_r.at[k, d], to, c, z, x))

    for dy in range(NY):
        ys = wrap(y - dy, NY)
        total = zsend[z, ys].astype(F32)
        for d in range(1, NZ):
            part = zrecv.at[d, ys]
            remote(part, part, zs.at[d, dy], zr.at[d, dy], y, c, z, x).wait_recv()
            total = total + zrecv[d, ys].astype(F32)
        for k in range(NX):
            att[k, ys] = total[k * 8 : (k + 1) * 8]
    for d in range(1, NX):
        to = wrap(x + d, NX)
        go(remote(att.at[to], xrecv.at[x], xs.at[d], xr.at[d], y, c, z, to))
    xrecv[x] = att[x]
    for d in range(1, NX):
        part = xrecv.at[wrap(x - d, NX)]
        remote(part, part, xs.at[d], xr.at[d], y, c, z, x).wait_recv()
    for k in range(NX):
        low = 256 if k == NX - 1 else 0
        at = k * CW
        wide = CW - low
        hidden[:, at : at + wide] = (
            xrecv[k].reshape(NY * 8, CW)[:, low:]
            + res_y[:, :, at : at + wide].reshape(NY * 8, wide)
        )
    held = hidden[...]
    squares[y] = jnp.broadcast_to(jnp.sum(held * held, axis=1, keepdims=True), (NY * 8, 128))
    for d in range(1, NY):
        go(remote(squares.at[y], squares.at[y], qs.at[d], qr.at[d], wrap(y + d, NY), c, z, x))
    for d in range(1, NY):
        part = squares.at[wrap(y - d, NY)]
        remote(part, part, qs.at[d], qr.at[d], y, c, z, x).wait_recv()
    mean = (squares[0] + squares[1] + squares[2] + squares[3])[:, :1] * (1.0 / D)
    tokens[z] = (held * lax.rsqrt(mean + NORM_EPS) * gain[...]).astype(BF16)
    for d in (4, 3, 5, 2, 6, 1, 7):
        go(remote(tokens.at[z], tokens.at[z], ts.at[d], tr.at[d], y, c, wrap(z + d, NZ), x))
    for d in range(1, NZ):
        part = tokens.at[wrap(z - d, NZ)]
        remote(part, part, ts.at[d], tr.at[d], y, c, z, x).wait_recv()
    table = tokens[...].reshape(NZ * 32, DY)
    for d in (2, 1, 3, 0):
        to = wrap(x + d, NX)
        disp[to] = jnp.dot(choose[to], table, preferred_element_type=F32).astype(BF16)
        if d:
            go(remote(disp.at[to], rows.at[x], ds.at[d], dr.at[d], y, c, z, to))
        else:
            last = pltpu.make_async_copy(disp.at[to], rows.at[x], loc.at[3])
            last.start()
            own.append(last)

    for d in (1, 3, 2):
        src = wrap(y - d, NY) * 2 + c
        for k, dst in enumerate((wg_all, wu_all, wd_all)):
            part = dst.at[src]
            remote(part, part, w_s.at[k, d], w_r.at[k, d], y, c, z, x).wait_recv()
            go(remote(part, part, f_s.at[k, d], f_r.at[k, d], y, other, z, x))
    for d in range(1, NX):
        part = rows.at[wrap(x - d, NX)]
        remote(part, part, ds.at[d], dr.at[d], y, c, z, x).wait_recv()
    for d in range(NY):
        src = wrap(y - d, NY) * 2 + other
        for k, dst in enumerate((wg_all, wu_all, wd_all)):
            part = dst.at[src]
            remote(part, part, f_s.at[k, d], f_r.at[k, d], y, c, z, x).wait_recv()
    for copy in own:
        copy.wait()
    for copy in started:
        copy.wait_send()


def project_and_dispatch(ho, op_all, res_y, gain, choose, wg, wu, wd):
    return pl.pallas_call(
        mid_kernel,
        out_shape=(
            jax.ShapeDtypeStruct((NY * 8, DY), F32),
            jax.ShapeDtypeStruct((NX, 96, DY), BF16),
            jax.ShapeDtypeStruct((8, DY, 128), BF16),
            jax.ShapeDtypeStruct((8, DY, 128), BF16),
            jax.ShapeDtypeStruct((8, 128, DY), BF16),
        ),
        in_specs=[VMEM] * 5 + [ANY] * 3,
        out_specs=(VMEM, ANY, ANY, ANY, ANY),
        scratch_shapes=[
            pltpu.VMEM((NY, NX, 256, 256), BF16),
            pltpu.VMEM((NZ, NY, 32, CW), BF16),
            pltpu.VMEM((NZ, NY, 32, CW), BF16),
            pltpu.VMEM((NX, NY, 8, CW), F32),
            pltpu.VMEM((NX, NY, 8, CW), F32),
            pltpu.VMEM((NY, NY * 8, 128), F32),
            pltpu.VMEM((NZ, NY * 8, DY), BF16),
            pltpu.VMEM((NX, 96, DY), BF16),
            DMA((4,)),
            DMA((16,)), DMA((16,)),
            DMA((NZ, NY)), DMA((NZ, NY)),
            DMA((NX,)), DMA((NX,)),
            DMA((NY,)), DMA((NY,)),
            DMA((NZ,)), DMA((NZ,)),
            DMA((NX,)), DMA((NX,)),
            DMA((3, NY)), DMA((3, NY)),
            DMA((3, NY)), DMA((3, NY)),
        ],
        compiler_params=pltpu.CompilerParams(
            collective_id=1, has_side_effects=True, vmem_limit_bytes=40 << 20
        ),
        name="project_and_dispatch",
    )(ho, op_all, res_y, gain, choose, wg, wu, wd)


def expert_kernel(
    rows, combine, hidden, wg_all, wu_all, wd_all,
    out,
    w_in, w_out, gsend, grecv, act, dout, back, zsend, zrecv, fin, orecv,
    loc, gs, gr, as_, ar, bs, br, zs, zr, os_, or_,
):
    y, c, z, x = place()
    fetch = []
    for k in range(8):
        at = pl.ds(k * 128, 128)
        fetch.append(pltpu.make_async_copy(wg_all.at[k], w_in.at[:, at], loc.at[0, k]))
        fetch.append(
            pltpu.make_async_copy(wu_all.at[k], w_in.at[:, pl.ds(FF + k * 128, 128)], loc.at[1, k])
        )
    for k in range(8):
        fetch.append(pltpu.make_async_copy(wd_all.at[k], w_out.at[pl.ds(k * 128, 128), :], loc.at[2, k]))
    for copy in fetch:
        copy.start()
    meet(y_peers(y, c, z, x) + z_peers(y, c, z, x) + x_peers(y, c, z, x))
    started = []

    def go(copy):
        copy.start()
        started.append(copy)

    for copy in fetch:
        copy.wait()
    every = rows[...].reshape(NX * 96, DY)

    def inward(j, _):
        at = pl.ds(pl.multiple_of(j * 512, 512), 512)
        part = jnp.dot(every, w_in[:, at], preferred_element_type=F32).astype(BF16)
        for k in range(NX):
            gsend[k, :, at] = part[k * 96 : (k + 1) * 96]
        return 0

    lax.fori_loop(0, 2 * FF // 512, inward, 0)
    for d in (2, 1, 3):
        to = wrap(y + d, NY)
        go(remote(gsend.at[to], grecv.at[d], gs.at[d], gr.at[d], to, c, z, x))
    summed = gsend[y].astype(F32)
    for d in (1, 3, 2):
        part = grecv.at[d]
        remote(part, part, gs.at[d], gr.at[d], y, c, z, x).wait_recv()
        summed = summed + grecv[d].astype(F32)
    gate = summed[:, :FF]
    act[y] = (gate / (1.0 + jnp.exp(-gate)) * summed[:, FF:]).astype(BF16)
    for d in (2, 1, 3):
        go(remote(act.at[y], act.at[y], as_.at[d], ar.at[d], wrap(y + d, NY), c, z, x))
    for d in (1, 3, 2):
        part = act.at[wrap(y - d, NY)]
        remote(part, part, as_.at[d], ar.at[d], y, c, z, x).wait_recv()
    acts = act[...].reshape(NX * 96, FF)

    def outward(j, _):
        at = pl.ds(pl.multiple_of(j * 256, 256), 256)
        part = jnp.dot(acts, w_out[:, at], preferred_element_type=F32).astype(BF16)
        for k in range(NX):
            dout[k, :, at] = part[k * 96 : (k + 1) * 96]
        return 0

    lax.fori_loop(0, DY // 256, outward, 0)
    for d in (2, 1, 3):
        to = wrap(x + d, NX)
        go(remote(dout.at[to], back.at[x], bs.at[d], br.at[d], y, c, z, to))
    back[x] = dout[x]
    for d in (1, 3, 2):
        part = back.at[wrap(x - d, NX)]
        remote(part, part, bs.at[d], br.at[d], y, c, z, x).wait_recv()

    def gather(j, _):
        at = pl.ds(pl.multiple_of(j * 256, 256), 256)
        part = jnp.dot(
            combine[...], back[:, :, at].reshape(NX * 96, 256), preferred_element_type=F32
        ).astype(BF16)
        for k in range(NZ):
            zsend[k, :, at] = part[k * 32 : (k + 1) * 32]
        return 0

    lax.fori_loop(0, DY // 256, gather, 0)
    for d in (4, 3, 5, 2, 6, 1, 7):
        to = wrap(z + d, NZ)
        go(remote(zsend.at[to], zrecv.at[d], zs.at[d], zr.at[d], y, c, to, x))
    total = hidden[...] + zsend[z].astype(F32)
    for d in range(1, NZ):
        part = zrecv.at[d]
        remote(part, part, zs.at[d], zr.at[d], y, c, z, x).wait_recv()
        total = total + zrecv[d].astype(F32)
    for k in range(NY):
        fin[k] = total[k * 8 : (k + 1) * 8]
    for d in range(1, NY):
        to = wrap(y + d, NY)
        go(remote(fin.at[to], orecv.at[y], os_.at[d], or_.at[d], to, c, z, x))
    orecv[y] = fin[y]
    for d in range(1, NY):
        part = orecv.at[wrap(y - d, NY)]
        remote(part, part, os_.at[d], or_.at[d], y, c, z, x).wait_recv()
    for k in range(NY):
        out[:, k * DY : (k + 1) * DY] = orecv[k]
    for copy in started:
        copy.wait_send()


def run_experts(rows, combine, hidden, wg_all, wu_all, wd_all):
    return pl.pallas_call(
        expert_kernel,
        out_shape=jax.ShapeDtypeStruct((8, D), F32),
        in_specs=[VMEM] * 3 + [ANY] * 3,
        out_specs=VMEM,
        scratch_shapes=[
            pltpu.VMEM((DY, 2 * FF), BF16),
            pltpu.VMEM((FF, DY), BF16),
            pltpu.VMEM((NY, 96, 2 * FF), BF16),
            pltpu.VMEM((NY, 96, 2 * FF), BF16),
            pltpu.VMEM((NY, 96, FF), BF16),
            pltpu.VMEM((NX, 96, DY), BF16),
            pltpu.VMEM((NX, 96, DY), BF16),
            pltpu.VMEM((NZ, NY * 8, DY), BF16),
            pltpu.VMEM((NZ, NY * 8, DY), BF16),
            pltpu.VMEM((NY, 8, DY), F32),
            pltpu.VMEM((NY, 8, DY), F32),
            DMA((3, 8)),
            DMA((NY,)), DMA((NY,)),
            DMA((NY,)), DMA((NY,)),
            DMA((NX,)), DMA((NX,)),
            DMA((NZ,)), DMA((NZ,)),
            DMA((NY,)), DMA((NY,)),
        ],
        compiler_params=pltpu.CompilerParams(
            collective_id=2, has_side_effects=True, vmem_limit_bytes=48 << 20
        ),
        name="run_experts",
    )(rows, combine, hidden, wg_all, wu_all, wd_all)


def on_device(
    queries,
    latent_cache,
    ancestors,
    value_up,
    out_proj,
    residual,
    norm_gain,
    routes,
    gates,
    w_gate,
    w_up,
    w_down,
):
    y, c, z, x = place()
    flat = routes.reshape(-1)
    earlier = jnp.arange(64)[:, None] > jnp.arange(64)[None, :]
    slots = jnp.sum(
        jnp.logical_and(earlier, flat[:, None] == flat[None, :]).astype(jnp.int32), axis=1
    )
    positions = (flat * CAP + slots).reshape(8, TOP).astype(F32)
    meta = jnp.concatenate([positions, gates, jnp.zeros((8, 128 - 2 * TOP), F32)], axis=1)
    lat_all, op_all, meta_all, res_y = exchange_first(
        latent_cache, out_proj, meta, residual.astype(F32)
    )
    live = jnp.concatenate(
        [jnp.repeat((ancestors >= 0).astype(F32), BLK, axis=1), jnp.ones((4, BLK), F32)], axis=1
    )
    head_out = attend(
        ancestors,
        queries.transpose(1, 0, 2),
        lat_all.reshape(32, BLK, LAT + ROPE),
        live,
        value_up,
    )
    table = meta_all.reshape(256, 128)
    where = table[:, :TOP].astype(jnp.int32)
    row = jnp.arange(384, dtype=jnp.int32)
    wanted = (z * NX + row // 96) * CAP + row % CAP
    block = (row % 96) // CAP
    same = block[:, None] == (jnp.arange(256, dtype=jnp.int32) // 8)[None, :]
    hit = jnp.logical_and(where.T[None, :, :] == wanted[:, None, None], same[:, None, :])
    choose = jnp.any(hit, axis=1).astype(BF16).reshape(NX, 96, 256)
    hit_t = jnp.logical_and(where[:, :, None] == wanted[None, None, :], same.T[:, None, :])
    combine = jnp.sum(jnp.where(hit_t, table[:, TOP : 2 * TOP, None], 0.0), axis=1).astype(BF16)
    gain = lax.dynamic_slice(norm_gain, (y * DY,), (DY,)).astype(F32).reshape(1, DY)
    hidden, rows, wg_all, wu_all, wd_all = project_and_dispatch(
        head_out, op_all, res_y, gain, choose, w_gate[0], w_up[0], w_down[0]
    )
    final = run_experts(rows, combine, hidden, wg_all, wu_all, wd_all)
    return final.astype(BF16)


def solution(mesh):
    placed = (
        P("seq", "exp", None),
        P("seq", None, None),
        P("seq", None),
        P("exp", None, None),
        P("exp", None),
        P(("seq", "exp"), None),
        P(),
        P(("seq", "exp"), None),
        P(("seq", "exp"), None),
        P("exp", None, "seq"),
        P("exp", None, "seq"),
        P("exp", "seq", None),
    )
    return jax.shard_map(
        on_device, mesh=mesh, in_specs=placed, out_specs=P(("seq", "exp"), None), check_vma=False
    )
```

time: 730 us -> 277 us (0.38)
  waiting for transfers between devices: 519 us -> 0 us
  Pallas kernels: 0 us -> 250 us
  local copies, waits for them, and re-layouts: 96 us -> 11.9 us
  blocking collectives: 47.7 us -> 0 us
  matrix products: 31.8 us -> 0 us
  between operations: 14 us -> 0.16 us
  starting transfers between devices: 10.5 us -> 0 us
    pallas_call x0 -> x4, Pallas kernels: none -> 250 us  [the longest x1 127 us: project_and_dispatch(): pl.pallas_call(mid_kernel, out_shape=(jax.ShapeDtypeStruct((NY * 8, DY),...]
    reduce_scatter x1 -> x0, waiting for transfers between devices: 219 us -> none  [on_device(): lax.psum_scatter(jnp.dot(rows, out_proj, preferred_element_type=jnp.float...]
    unnamed x5 -> x0, waiting for transfers between devices: 168 us -> none
    all_gather x2 -> x0, waiting for transfers between devices: 90.6 us -> none  [the longest x1 60.5 us: on_device(): piece = lax.all_gather(arrived, 'seq', axis=0, tiled=True)]
    all_to_all x1 -> x0, blocking collectives: 47.7 us -> none  [on_device(): lax.all_to_all(buffer, 'exp', split_axis=0, concat_axis=0, tiled=True)]
    all_to_all x1 -> x0, waiting for transfers between devices: 40.8 us -> none  [on_device(): lax.all_to_all(summed_rows, 'exp', split_axis=0, concat_axis=0, tiled=True)]
    dot_general x7 -> x0, matrix products: 31.8 us -> none  [the longest x1 17.3 us: on_device(): jnp.dot(act, down_local, preferred_element_type=jnp.float32)]
    reshape x3 -> x2, local copies, waits for them, and re-layouts: 28.4 us -> 0.68 us  [the longest x1 0.6 us: on_device(): lax.dynamic_slice(norm_gain, (y * DY,), (DY,)).astype(F32).reshape(1, DY)]
  transfers between devices with their start and end apart: 5 -> 0, of which waited for: 5 -> 0; matrix products, arithmetic and copies ran while one was open for 1% -> 0% of each run, Pallas kernels for 0% -> 0%
where the time goes in v1:
time: 277 us; the launch traced here: 276 us
  Pallas kernels  250 us (90%)
  other arithmetic  13.9 us (5%)
  local copies, waits for them, and re-layouts  11.9 us (4%)
    pallas_call x1, Pallas kernels, project_and_dispatch(): pl.pallas_call(mid_kernel, out_shape=(jax.ShapeDtypeStruct((NY * 8, DY),...  127 us
    pallas_call x1, Pallas kernels, run_experts(): pl.pallas_call(expert_kernel, out_shape=jax.ShapeDtypeStruct((8, D), F32)...  86.2 us
    pallas_call x1, Pallas kernels, exchange_first(): pl.pallas_call(pre_kernel, out_shape=(jax.ShapeDtypeStruct((8,) + lat.sha...  32.5 us
    unnamed x27, local copies, waits for them, and re-layouts  10.1 us

profile of v1, /device:TPU:32, one launch (start us, length us, event | category | flops | bytes accessed | tf_op | source)
XLA Modules:
  0.0 275.6 jit_solution(10735963108817796295)
XLA Ops:
  0.0 0.0 copy-start.10
  0.0 0.8 eq.72
  0.8 0.2 convert_reduce_fusion
  1.0 0.1 pad.3.clone
  1.1 0.6 fusion.7
  1.7 0.7 compare_convert_fusion
  2.3 0.1 reduce_sum.21
  2.4 0.7 add_convert_fusion
  3.1 1.4 maximum_maximum_fusion.meta
  4.5 0.8 dynamic-slice_convert_fusion
  5.2 0.6 reshape.156.gain
  5.8 0.1 broadcast_in_dim.13
  5.9 0.1 reshape.151
  6.0 0.8 broadcast_compare_fusion
  6.8 0.8 broadcast_compare_fusion.1
  7.5 1.6 convert_element_type.31.res
  9.1 1.4 copy.15
  10.5 0.0 copy-start.1
  10.5 32.5 %exchange_first.1 = (bf16[8,4,64,576]{3,2,1,0:T(8,128)(2,1)}, bf16[4,256,512]{2,1,0:T(8,128)(2,1)}, f32[8,4,8,128]{3,2,1,0:T(8,128)}, f32[4,8,1792]{2,1,0:T(8,128)}) custom-call(bf16[4,64,576]{2,1,0:T(8,128)(2,1)} %lat.1, bf16[256,7168]{1,0:T(8,128)(2,1)} %outp.1, f32[8,128]{1,0:T(8,128)} %maximum_maximum_fusion.meta, f32[8,7168]{1,0:T(8,128)} %convert_element_type.31.res), custom_call_target="tpu_custom_call" | custom-call | tf_op jit(solution)/shard_map/exchange_first/pallas_call | solution.py:152
  43.0 0.0 copy-start.12
  43.0 0.0 copy-done.10
  43.0 0.0 copy-start
  43.0 1.7 copy-done
  44.7 0.0 copy-start.7
  44.7 0.9 copy-done.7
  45.7 0.0 copy-start.11
  45.7 0.0 copy-start.4
  45.7 3.6 %attend.1.ho = bf16[256,256]{1,0:T(8,128)(2,1)S(1)} custom-call(s32[4,8]{1,0:T(4,128)S(1)} %copy-done.10, bf16[2,256,576]{2,1,0:T(8,128)(2,1)S(1)} %bitcast.10, bf16[32,64,576]{2,1,0:T(8,128)(2,1)S(1)} %bitcast.9, f32[4,576]{1,0:T(4,128)S(1)} %concatenate.7.live, bf16[2,512,128]{2,1,0:T(8,128)(2,1)S(1)} %copy-done.7), custom_call_target="tpu_custom_call" | custom-call | tf_op jit(solution)/shard_map/attend/pallas_call | solution.py:208
  49.2 0.0 copy-done.11
  49.3 0.0 copy-start.5
  49.3 0.1 slice_convert_fusion
  49.4 0.5 copy-done.5
  49.9 0.0 copy-done.12
  49.9 2.7 select_reduce_fusion.combine
  52.6 0.1 copy.16
  52.6 3.0 %and_reduce_fusion = pred[384,256]{1,0:T(8,128)(4,1)S(1)} fusion(s32[8,256]{1,0:T(8,128)S(1)} %copy.16, s32[384]{0:T(512)} %fusion.7, pred[384,256]{1,0:T(8,128)(4,1)} %broadcast_compare_fusion.1), kind=kLoop, calls=%fused_computation.1 | loop fusion | flops 2260992 | bytes 206336 | tf_op jit(solution)/shard_map/reduce_or | solution.py:576
  55.7 0.0 copy-done.1
  55.7 0.0 copy-done.4
  55.7 0.0 copy-start.2
  55.7 1.5 copy-done.2
  57.2 0.0 copy-start.3
  57.2 1.5 copy-done.3
  58.7 0.9 copy-done.6
  59.6 0.9 copy-done.8
  60.6 0.7 copy-done.9
  61.3 127.5 %project_and_dispatch.1 = (f32[32,1792]{1,0:T(8,128)S(1)}, bf16[4,96,1792]{2,1,0:T(8,128)(2,1)S(1)}, bf16[8,1792,128]{2,1,0:T(8,128)(2,1)S(1)}, bf16[8,1792,128]{2,1,0:T(8,128)(2,1)}, bf16[8,128,1792]{2,1,0:T(8,128)(2,1)}) custom-call(bf16[256,256]{1,0:T(8,128)(2,1)S(1)} %copy-done.6, bf16[4,256,512]{2,1,0:T(8,128)(2,1)S(1)} %copy-done.4, ...), custom_call_target="tpu_custom_call" | custom-call | tf_op jit(solution)/shard_map/project_and_dispatch/pallas_call | solution.py:362
  188.8 86.2 %run_experts.1 = f32[8,7168]{1,0:T(8,128)S(1)} custom-call(bf16[4,96,1792]{2,1,0:T(8,128)(2,1)S(1)} %get-tuple-element.18.rows, bf16[256,384]{1,0:T(8,128)(2,1)S(1)} %select_reduce_fusion.combine, f32[32,1792]{1,0:T(8,128)S(1)} %get-tuple-element.19.hidden, bf16[8,1792,128]{2,1,0:T(8,128)(2,1)S(1)} %get-tuple-element.20.wg_all, ...), custom_call_target="tpu_custom_call" | custom-call | tf_op jit(solution)/shard_map/run_experts/pallas_call | solution.py:503
  275.0 0.7 convert_element_type.37
  (8 shorter events, 0.1 us)
Async XLA Ops:
  0.0 43.0 %copy-start.10 = (s32[4,8]{1,0:T(4,128)S(1)}, s32[4,8]{1,0:T(4,128)}, u32[]{:S(2)}) copy-start(s32[4,8]{1,0:T(4,128)} %anc.1) | copy-start | bytes 388
  10.5 45.2 %copy-start.1 = (bf16[1,7168,128]{2,1,0:T(8,128)(2,1)S(1)}, bf16[1,7168,128]{2,1,0:T(8,128)(2,1)}, u32[]{:S(2)}) copy-start(bf16[1,7168,128]{2,1,0:T(8,128)(2,1)} %param.21) | copy-start | bytes 5505028
  43.0 7.0 %copy-start.12 = (s32[384]{0:T(512)S(1)}, s32[384]{0:T(512)}, u32[]{:S(2)}) copy-start(s32[384]{0:T(512)} %fusion.7) | copy-start | bytes 4612
  43.0 1.7 copy-start
  44.7 0.9 copy-start.7
  45.7 3.6 %copy-start.11 = (f32[8,4,8,128]{3,2,1,0:T(8,128)S(1)}, f32[8,4,8,128]{3,2,1,0:T(8,128)}, u32[]{:S(2)}) copy-start(f32[8,4,8,128]{3,2,1,0:T(8,128)} %get-tuple-element.17) | copy-start | bytes 393220
  45.7 10.1 %copy-start.4 = (bf16[4,256,512]{2,1,0:T(8,128)(2,1)S(1)}, bf16[4,256,512]{2,1,0:T(8,128)(2,1)}, u32[]{:S(2)}) copy-start(bf16[4,256,512]{2,1,0:T(8,128)(2,1)} %get-tuple-element.15.op_all) | copy-start | bytes 3145732
  49.3 0.7 copy-start.5
  55.7 1.5 copy-start.2
  57.2 1.5 copy-start.3
  58.7 0.9 copy-start.6
  59.6 0.9 copy-start.8
  60.6 0.7 copy-start.9

commit v2 on v0

v2 whole, which is shorter than its diff:
```python
import jax
import jax.numpy as jnp
from jax import lax
from jax.experimental import pallas as pl
from jax.experimental.pallas import tpu as pltpu
from jax.sharding import PartitionSpec as P

D = 7168
LAT = 512
ROPE = 64
HD = 128
BLK = 64
ANC = 8
TOP = 8
CAP = 3
NY, NZ, NX = 4, 8, 4
DY = D // NY
CW = 512
FF = 1024
HALF = 48
UNNAMED = 99.0
NORM_EPS = 1e-6
MASKED = -1e30
F32 = jnp.float32
BF16 = jnp.bfloat16
ANY = pl.BlockSpec(memory_space=pl.ANY)
VMEM = pl.BlockSpec(memory_space=pltpu.VMEM)
SMEM = pl.BlockSpec(memory_space=pltpu.SMEM)
DMA = pltpu.SemaphoreType.DMA


def place():
    s = lax.axis_index("seq")
    e = lax.axis_index("exp")
    return lax.div(s, 2), lax.rem(s, 2), lax.div(e, NX), lax.rem(e, NX)


def wrap(value, count):
    return lax.rem(value + count, count)


def meet(peers):
    barrier = pltpu.get_barrier_semaphore()
    for y, c, z, x in peers:
        pl.semaphore_signal(
            barrier,
            inc=1,
            device_id=(y * 2 + c, z * NX + x),
            device_id_type=pl.DeviceIdType.MESH,
        )
    pl.semaphore_wait(barrier, len(peers))


class Links:
    def __init__(self, y, c, z, x):
        self.at = (y, c, z, x)
        self.started = []

    def copy(self, src, dst, send_sem, recv_sem, y=None, c=None, z=None, x=None):
        here = self.at
        y, c, z, x = (own if new is None else new for new, own in zip((y, c, z, x), here))
        return pltpu.make_async_remote_copy(
            src_ref=src,
            dst_ref=dst,
            send_sem=send_sem,
            recv_sem=recv_sem,
            device_id=(y * 2 + c, z * NX + x),
            device_id_type=pl.DeviceIdType.MESH,
        )

    def send(self, src, dst, send_sem, recv_sem, **to):
        copy = self.copy(src, dst, send_sem, recv_sem, **to)
        copy.start()
        self.started.append(copy)

    def arrived(self, dst, send_sem, recv_sem):
        self.copy(dst, dst, send_sem, recv_sem).wait_recv()

    def finish(self):
        for copy in self.started:
            copy.wait_send()


def ring_gather(links, axis, count, me, view, half, send_sem, recv_sem):
    last = count // 2
    for step in range(1, last + 1):
        new = []
        for way, sign in enumerate((1, -1)):
            k = -sign * (step - 1)
            if step > 1:
                links.arrived(view(k, 0), send_sem.at[way, step - 1], recv_sem.at[way, step - 1])
                new.append(k)
            src, dst = view(k, 0), view(k, sign)
            if step == last:
                src, dst = half(src, way), half(dst, way)
            links.send(
                src, dst, send_sem.at[way, step], recv_sem.at[way, step],
                **{axis: wrap(me + sign, count)},
            )
        if new:
            yield new
    for way, sign in enumerate((1, -1)):
        links.arrived(
            half(view(-sign * last, 0), way), send_sem.at[way, last], recv_sem.at[way, last]
        )
    yield [last]


def ring_reduce(links, axis, count, me, own, sent, got, send_sem, recv_sem):
    last = count // 2
    for step in range(1, last + 1):
        yield step
        for h in range(2):
            for way, sign in enumerate((1, -1)):
                if step == 1 and h != way:
                    continue
                value = own(sign * (last + 1 - step), h)
                if step > 2 or (step == 2 and h == way):
                    links.arrived(
                        got.at[way, step - 1, h],
                        send_sem.at[way, step - 1, h],
                        recv_sem.at[way, step - 1, h],
                    )
                    value = value + got[way, step - 1, h].astype(F32)
                sent[way, step, h] = value.astype(BF16)
                links.send(
                    sent.at[way, step, h], got.at[way, step, h],
                    send_sem.at[way, step, h], recv_sem.at[way, step, h],
                    **{axis: wrap(me + sign, count)},
                )
    for h in range(2):
        for way in range(2):
            links.arrived(
                got.at[way, last, h], send_sem.at[way, last, h], recv_sem.at[way, last, h]
            )


def drain(steps):
    for _ in steps:
        pass


def routing_table(routes, gates):
    lane = lax.broadcasted_iota(jnp.int32, (8, 128), 1)
    gate = jnp.zeros((8, 128), F32)
    named = jnp.zeros((8, 128), F32)
    for k in range(TOP):
        expert = routes[:, k : k + 1]
        gate = gate + jnp.where(expert == lane, gates[:, k : k + 1], 0.0)
        named = named + jnp.where(expert == lane - 32, 1.0, 0.0)
    row = lax.broadcasted_iota(jnp.int32, (8, 8), 0)
    col = lax.broadcasted_iota(jnp.int32, (8, 8), 1)
    before = jnp.dot((col < row).astype(F32), named, preferred_element_type=F32)
    return jnp.where(lane < 32, gate, jnp.where(named > 0.5, before, UNNAMED))


def matches(table, z):
    lane = lax.broadcasted_iota(jnp.int32, (128, 128), 1)
    row = lax.broadcasted_iota(jnp.int32, (128, NX * HALF), 1)
    token = lax.broadcasted_iota(jnp.int32, (128, NX * HALF), 0)
    slot = jnp.zeros((128, NX * HALF), F32)
    gate = jnp.zeros((128, NX * HALF), F32)
    for k in range(NX):
        expert = z * NX + k
        gate_col = jnp.sum(jnp.where(lane == expert, table, 0.0), axis=1, keepdims=True)
        slot_col = jnp.sum(jnp.where(lane == expert + 32, table, 0.0), axis=1, keepdims=True)
        mine = jnp.logical_and(row >= k * HALF, row < (k + 1) * HALF)
        slot = jnp.where(mine, slot_col, slot)
        gate = jnp.where(mine, gate_col, gate)
    inner = lax.rem(row, HALF)
    hit = jnp.logical_and(
        lax.div(token, 8) == lax.div(inner, CAP), slot == lax.rem(inner, CAP).astype(F32)
    )
    return jnp.where(hit, 1.0, 0.0).astype(BF16), jnp.where(hit, gate, 0.0).astype(BF16)


def attend(g, s, anc, live, q, lat, vup, keys):
    width = (ANC + 1) * BLK
    col = lax.broadcasted_iota(jnp.int32, (2 * BLK, width), 1)
    row = lax.rem(lax.broadcasted_iota(jnp.int32, (2 * BLK, width), 0), BLK)
    for a in range(ANC):
        keys[a * BLK : (a + 1) * BLK, :] = lat[jnp.maximum(anc[g, a], 0)]
    keys[ANC * BLK :, :] = lat[s * 4 + g]
    query = q[:, g * BLK : (g + 1) * BLK, :].reshape(2 * BLK, LAT + ROPE)
    scores = lax.dot_general(
        query, keys[...], (((1,), (1,)), ((), ())), preferred_element_type=F32
    ) * ((HD + ROPE) ** (-0.5))
    mask = jnp.logical_and(row >= col - ANC * BLK, live[g : g + 1, :] > 0.5)
    highest = jnp.max(jnp.where(mask, scores, MASKED), axis=1, keepdims=True)
    weights = jnp.where(mask, jnp.exp(scores - highest), 0.0)
    total = jnp.sum(weights, axis=1, keepdims=True)
    summed = jnp.dot(weights.astype(BF16), keys[:, :LAT], preferred_element_type=F32)
    latent = (summed / total).astype(BF16)
    return jnp.concatenate(
        [
            jnp.dot(latent[h * BLK : (h + 1) * BLK], vup[h], preferred_element_type=F32)
            for h in range(2)
        ],
        axis=1,
    ).astype(BF16)


def layer_kernel(
    anc, anc_rows, q, vup, routes, gates, res, gain, lat_in, outp, wg, wu, wd,
    out,
    lat, keys, meta, meta_all, res32, res_y, op_all, ho_a, ho_b, partial, a_sent, a_got,
    att, xrecv, hidden, squares, tokens, choose, combine, disp, rows, w_in, w_out,
    gsend, g_sent, g_got, act, dout, back, comb, c_sent, c_got, fin, orecv,
    loc, lat_s, lat_r, fwd_s, fwd_r, op_s, op_r, me_s, me_r, mz_s, mz_r, re_s, re_r,
    a1_s, a1_r, b1_s, b1_r, a2_s, a2_r, b2_s, b2_r, za_s, za_r, xa_s, xa_r, sq_s, sq_r,
    tk_s, tk_r, dp_s, dp_r, w_s, w_r, f_s, f_r, gy_s, gy_r, ac_s, ac_r, bk_s, bk_r,
    zc_s, zc_r, fo_s, fo_r,
):
    y, c, z, x = place()
    s = y * 2 + c
    other = 1 - c
    links = Links(y, c, z, x)
    send, arrived = links.send, links.arrived

    def weight_source(k, to):
        at = pl.ds(pl.multiple_of(to * DY, 128), DY)
        return (wg.at[at, :], wu.at[at, :], wd.at[:, at])[k]

    def weight_place(k, src):
        if k == 2:
            return w_out.at[pl.ds(pl.multiple_of(src * 128, 128), 128), :]
        return w_in.at[:, pl.ds(pl.multiple_of(k * FF + src * 128, 128), 128)]

    def op_columns(to):
        start = pl.multiple_of(y * DY + jnp.minimum(to * CW, DY - CW), 128)
        return outp.at[:, pl.ds(start, CW)]

    own = [
        pltpu.make_async_copy(lat_in, lat.at[pl.ds(s * 4, 4)], loc.at[0]),
        pltpu.make_async_copy(op_columns(x), op_all.at[x], loc.at[1]),
    ] + [
        pltpu.make_async_copy(weight_source(k, y), weight_place(k, s), loc.at[2 + k])
        for k in range(3)
    ]
    for copy in own:
        copy.start()
    meta[...] = routing_table(routes[...], gates[...])
    meta_all[1, y] = meta[...]
    res32[...] = res[...].astype(F32)
    meet(
        [(wrap(y + d, NY), c, z, x) for d in range(1, NY)]
        + [(y, c, wrap(z + d, NZ), x) for d in range(1, NZ)]
        + [(y, c, z, wrap(x + d, NX)) for d in range(1, NX)]
        + [(y, other, z, x)]
    )

    own[0].wait()

    def lat_view(k, shift):
        return lat.at[pl.ds((wrap(y + k, NY) * 2 + c) * 4, 4)]

    lat_ring = ring_gather(
        links, "y", NY, y, lat_view, lambda ref, h: ref.at[pl.ds(h * 2, 2)], lat_s, lat_r
    )

    def forward(k):
        block = lat_view(k, 0)
        send(block, block, fwd_s.at[k % NY], fwd_r.at[k % NY], c=other)

    for d in range(1, NY):
        to = wrap(y + d, NY)
        send(meta, meta_all.at[1, y], me_s.at[d], me_r.at[d], y=to)
    first = next(lat_ring)
    forward(0)
    for k in first:
        forward(k)
    for d in range(1, NY):
        to = wrap(y + d, NY)
        part = res32.at[:, pl.ds(pl.multiple_of(to * DY, 128), DY)]
        send(part, res_y.at[y], re_s.at[d], re_r.at[d], y=to)
    for d in range(1, NX):
        to = wrap(x + d, NX)
        send(op_columns(to), op_all.at[x], op_s.at[d], op_r.at[d], x=to)
    for d in range(1, NY):
        arrived(meta_all.at[1, wrap(y - d, NY)], me_s.at[d], me_r.at[d])
    for d in range(1, NZ):
        send(meta_all.at[1], meta_all.at[(d + 1) % NZ], mz_s.at[d], mz_r.at[d], z=wrap(z + d, NZ))
    res_y[y] = res32[:, pl.ds(pl.multiple_of(y * DY, 128), DY)]
    area = lax.broadcasted_iota(jnp.int32, (ANC, (ANC + 1) * BLK), 1)
    slot_of = lax.broadcasted_iota(jnp.int32, (ANC, (ANC + 1) * BLK), 0)
    spread = (lax.div(area, BLK) == slot_of).astype(F32)
    live = jnp.dot((anc_rows[...] >= 0).astype(F32), spread, preferred_element_type=F32) + (
        lax.broadcasted_iota(jnp.int32, (4, (ANC + 1) * BLK), 1) >= ANC * BLK
    ).astype(F32)
    for new in lat_ring:
        for k in new:
            forward(k)
    for k in range(3):
        send(
            weight_source(k, y), weight_place(k, s), f_s.at[k, 0], f_r.at[k, 0], c=other
        )
    for d in (1, 3):
        to = wrap(y + d, NY)
        send(weight_source(2, to), weight_place(2, s), w_s.at[2, d], w_r.at[2, d], y=to)
    for k in range(NY):
        block = lat.at[pl.ds((wrap(y + k, NY) * 2 + other) * 4, 4)]
        arrived(block, fwd_s.at[k], fwd_r.at[k])

    for g in range(2):
        ho_a[y, x, g * BLK : (g + 1) * BLK, :] = attend(g, s, anc, live, q, lat, vup, keys)
    for d in range(1, NX):
        send(ho_a.at[y, x], ho_a.at[y, x], a1_s.at[d], a1_r.at[d], x=wrap(x + d, NX))
    for g in range(2):
        ho_b[x, y, g * BLK : (g + 1) * BLK, :] = attend(g + 2, s, anc, live, q, lat, vup, keys)
    for d in range(1, NY):
        send(ho_b.at[x, y], ho_b.at[x, y], b1_s.at[d], b1_r.at[d], y=wrap(y + d, NY))

    def pairs(ref, h):
        return ref.at[pl.ds(h * 2, 2)]

    a_ring = ring_gather(
        links, "y", NY, y, lambda k, shift: ho_a.at[wrap(y + k, NY)], pairs, a2_s, a2_r
    )
    b_ring = ring_gather(
        links, "x", NX, x, lambda k, shift: ho_b.at[wrap(x + k, NX)], pairs, b2_s, b2_r
    )
    for d in range(1, NX):
        arrived(ho_a.at[y, wrap(x - d, NX)], a1_s.at[d], a1_r.at[d])
    for d in range(1, NY):
        arrived(ho_b.at[x, wrap(y - d, NY)], b1_s.at[d], b1_r.at[d])
    next(a_ring)
    next(b_ring)
    for d in range(1, NZ):
        arrived(meta_all.at[(d + 1) % NZ], mz_s.at[d], mz_r.at[d])
    for h in range(2):
        pick, weigh = matches(meta_all[4 * h : 4 * h + 4].reshape(128, 128), z)
        choose[h] = pick
        combine[h] = weigh
    for d in range(1, NX):
        arrived(op_all.at[wrap(x - d, NX)], op_s.at[d], op_r.at[d])
    own[1].wait()
    drain(a_ring)
    drain(b_ring)
    for k in range(2):
        for d in (1, 3):
            to = wrap(y + d, NY)
            send(weight_source(k, to), weight_place(k, s), w_s.at[k, d], w_r.at[k, d], y=to)

    for n in range(NY):
        for low, block in ((0, lambda k: ho_a[n, k]), (4, lambda k: ho_b[k, n])):
            total = None
            for k in range(NX):
                part = jnp.dot(block(k), op_all[k], preferred_element_type=F32)
                total = part if total is None else total + part
            total = total.astype(BF16)
            for k in range(4):
                partial[low + k, n] = total[k * 32 : (k + 1) * 32]

    def attention_term(k, h):
        return partial[wrap(z + k, NZ), 2 * h : 2 * h + 2].astype(F32)

    drain(ring_reduce(links, "z", NZ, z, attention_term, a_sent, a_got, za_s, za_r))
    for h in range(2):
        total = (
            attention_term(0, h)
            + a_got[0, NZ // 2, h].astype(F32)
            + a_got[1, NZ // 2, h].astype(F32)
        )
        for k in range(NX):
            att[k, 2 * h : 2 * h + 2] = total[:, k * 8 : (k + 1) * 8]
    for d in range(1, NX):
        to = wrap(x + d, NX)
        send(att.at[to], xrecv.at[x], xa_s.at[d], xa_r.at[d], x=to)
    xrecv[x] = att[x]
    to = wrap(y + 2, NY)
    for k in range(3):
        send(weight_source(k, to), weight_place(k, s), w_s.at[k, 2], w_r.at[k, 2], y=to)
    for d in range(1, NY):
        arrived(res_y.at[wrap(y - d, NY)], re_s.at[d], re_r.at[d])
    for d in range(1, NX):
        arrived(xrecv.at[wrap(x - d, NX)], xa_s.at[d], xa_r.at[d])
    for k in range(NX):
        low = NX * CW - DY if k == NX - 1 else 0
        at, wide = k * CW, CW - low
        hidden[:, at : at + wide] = xrecv[k].reshape(NY * 8, CW)[:, low:] + res_y[
            :, :, at : at + wide
        ].reshape(NY * 8, wide)
    held = hidden[...]
    squares[y] = jnp.broadcast_to(jnp.sum(held * held, axis=1, keepdims=True), (NY * 8, 128))
    for d in range(1, NY):
        send(squares.at[y], squares.at[y], sq_s.at[d], sq_r.at[d], y=wrap(y + d, NY))
    for d in range(1, NY):
        arrived(squares.at[wrap(y - d, NY)], sq_s.at[d], sq_r.at[d])
    mean = (squares[0] + squares[1] + squares[2] + squares[3])[:, :1] * (1.0 / D)
    tokens[1] = (held * lax.rsqrt(mean + NORM_EPS) * gain[y]).astype(BF16)
    token_ring = ring_gather(
        links, "z", NZ, z,
        lambda k, shift: tokens.at[(1 - k + shift) % NZ],
        lambda ref, h: ref.at[pl.ds(h * 16, 16)],
        tk_s, tk_r,
    )

    def dispatch(h):
        table = tokens[4 * h : 4 * h + 4].reshape(128, DY)
        chosen = lax.dot_general(
            choose[h], table, (((0,), (0,)), ((), ())), preferred_element_type=F32
        ).astype(BF16)
        for k in range(NX):
            disp[h, k] = chosen[k * HALF : (k + 1) * HALF]
        for d in (2, 1, 3):
            to = wrap(x + d, NX)
            send(disp.at[h, to], rows.at[x, h], dp_s.at[h, d], dp_r.at[h, d], x=to)
        rows[x, h] = disp[h, x]

    def pass_on(k, d):
        block = weight_place(k, wrap(y - d, NY) * 2 + c)
        arrived(block, w_s.at[k, d], w_r.at[k, d])
        send(block, block, f_s.at[k, d], f_r.at[k, d], c=other)

    def from_other(k):
        own[2 + k].wait()
        for d in range(NY):
            block = weight_place(k, wrap(y - d, NY) * 2 + other)
            arrived(block, f_s.at[k, d], f_r.at[k, d])

    next(token_ring)
    next(token_ring)
    dispatch(0)
    next(token_ring)
    for k in (2, 0, 1):
        for d in (1, 3):
            pass_on(k, d)
    drain(token_ring)
    dispatch(1)
    for k in range(2):
        pass_on(k, 2)
    for k in range(2):
        from_other(k)

    for h in range(2):
        for d in range(1, NX):
            arrived(rows.at[wrap(x - d, NX), h], dp_s.at[h, d], dp_r.at[h, d])

        def inward(j, _):
            at = pl.ds(pl.multiple_of(j * 512, 512), 512)
            part = jnp.dot(
                rows[:, h].reshape(NX * HALF, DY), w_in[:, at], preferred_element_type=F32
            ).astype(BF16)
            for k in range(NX):
                gsend[k, h, :, at] = part[k * HALF : (k + 1) * HALF]
            return 0

        lax.fori_loop(0, 2 * FF // 512, inward, 0)

    def inward_term(k, h):
        return gsend[wrap(y + k, NY), h].astype(F32)

    drain(ring_reduce(links, "y", NY, y, inward_term, g_sent, g_got, gy_s, gy_r))
    for h in range(2):
        total = (
            inward_term(0, h)
            + g_got[0, NY // 2, h].astype(F32)
            + g_got[1, NY // 2, h].astype(F32)
        )
        gate = total[:, :FF]
        act[y, h] = (gate / (1.0 + jnp.exp(-gate)) * total[:, FF:]).astype(BF16)
    act_ring = ring_gather(
        links, "y", NY, y, lambda k, shift: act.at[wrap(y + k, NY)], lambda ref, h: ref.at[h],
        ac_s, ac_r,
    )
    next(act_ring)
    pass_on(2, 2)
    from_other(2)
    drain(act_ring)

    for h in (1, 0):
        def outward(j, _):
            at = pl.ds(pl.multiple_of(j * 256, 256), 256)
            part = jnp.dot(
                act[:, h].reshape(NX * HALF, FF), w_out[:, at], preferred_element_type=F32
            ).astype(BF16)
            for k in range(NX):
                dout[h, k, :, at] = part[k * HALF : (k + 1) * HALF]
            return 0

        lax.fori_loop(0, DY // 256, outward, 0)
        for d in (2, 1, 3):
            to = wrap(x + d, NX)
            send(dout.at[h, to], back.at[h, x], bk_s.at[h, d], bk_r.at[h, d], x=to)
        back[h, x] = dout[h, x]

    def weigh_rows(h):
        for d in range(1, NX):
            arrived(back.at[h, wrap(x - d, NX)], bk_s.at[h, d], bk_r.at[h, d])

        def gather(j, _):
            at = pl.ds(pl.multiple_of(j * 256, 256), 256)
            part = jnp.dot(
                combine[h], back[h, :, :, at].reshape(NX * HALF, 256), preferred_element_type=F32
            )
            for k in range(4):
                comb[4 * h + k, :, at] = part[k * 32 : (k + 1) * 32]
            return 0

        lax.fori_loop(0, DY // 256, gather, 0)

    def token_term(k, h):
        return comb[(1 - k) % NZ, h * 16 : (h + 1) * 16]

    weigh_rows(1)
    for step in ring_reduce(links, "z", NZ, z, token_term, c_sent, c_got, zc_s, zc_r):
        if step == 3:
            weigh_rows(0)
    for h in range(2):
        total = (
            hidden[h * 16 : (h + 1) * 16]
            + token_term(0, h)
            + c_got[0, NZ // 2, h].astype(F32)
            + c_got[1, NZ // 2, h].astype(F32)
        )
        fin[2 * h] = total[:8]
        fin[2 * h + 1] = total[8:]
    for d in (2, 1, 3):
        to = wrap(y + d, NY)
        send(fin.at[to], orecv.at[y], fo_s.at[d], fo_r.at[d], y=to)
    orecv[y] = fin[y]
    for d in range(1, NY):
        arrived(orecv.at[wrap(y - d, NY)], fo_s.at[d], fo_r.at[d])
    for k in range(NY):
        out[:, k * DY : (k + 1) * DY] = orecv[k]
    links.finish()


def layer(*operands):
    def two(*shape):
        return [DMA(shape), DMA(shape)]

    return pl.pallas_call(
        layer_kernel,
        out_shape=jax.ShapeDtypeStruct((8, D), F32),
        in_specs=[SMEM] + [VMEM] * 7 + [ANY] * 5,
        out_specs=VMEM,
        scratch_shapes=[
            pltpu.VMEM((32, BLK, LAT + ROPE), BF16),
            pltpu.VMEM(((ANC + 1) * BLK, LAT + ROPE), BF16),
            pltpu.VMEM((8, 128), F32),
            pltpu.VMEM((NZ, NY, 8, 128), F32),
            pltpu.VMEM((8, D), F32),
            pltpu.VMEM((NY, 8, DY), F32),
            pltpu.VMEM((NX, 256, CW), BF16),
            pltpu.VMEM((NY, NX, 128, 256), BF16),
            pltpu.VMEM((NX, NY, 128, 256), BF16),
            pltpu.VMEM((NZ, NY, 32, CW), BF16),
            pltpu.VMEM((2, NZ // 2 + 1, 2, 2, 32, CW), BF16),
            pltpu.VMEM((2, NZ // 2 + 1, 2, 2, 32, CW), BF16),
            pltpu.VMEM((NX, NY, 8, CW), F32),
            pltpu.VMEM((NX, NY, 8, CW), F32),
            pltpu.VMEM((NY * 8, DY), F32),
            pltpu.VMEM((NY, NY * 8, 128), F32),
            pltpu.VMEM((NZ, NY * 8, DY), BF16),
            pltpu.VMEM((2, 128, NX * HALF), BF16),
            pltpu.VMEM((2, 128, NX * HALF), BF16),
            pltpu.VMEM((2, NX, HALF, DY), BF16),
            pltpu.VMEM((NX, 2, HALF, DY), BF16),
            pltpu.VMEM((DY, 2 * FF), BF16),
            pltpu.VMEM((FF, DY), BF16),
            pltpu.VMEM((NY, 2, HALF, 2 * FF), BF16),
            pltpu.VMEM((2, NY // 2 + 1, 2, HALF, 2 * FF), BF16),
            pltpu.VMEM((2, NY // 2 + 1, 2, HALF, 2 * FF), BF16),
            pltpu.VMEM((NY, 2, HALF, FF), BF16),
            pltpu.VMEM((2, NX, HALF, DY), BF16),
            pltpu.VMEM((2, NX, HALF, DY), BF16),
            pltpu.VMEM((NZ, NY * 8, DY), F32),
            pltpu.VMEM((2, NZ // 2 + 1, 2, 16, DY), BF16),
            pltpu.VMEM((2, NZ // 2 + 1, 2, 16, DY), BF16),
            pltpu.VMEM((NY, 8, DY), F32),
            pltpu.VMEM((NY, 8, DY), F32),
            DMA((5,)),
            *two(2, NY // 2 + 1),
            *two(NY),
            *two(NX),
            *two(NY),
            *two(NZ),
            *two(NY),
            *two(NX),
            *two(NY),
            *two(2, NY // 2 + 1),
            *two(2, NX // 2 + 1),
            *two(2, NZ // 2 + 1, 2),
            *two(NX),
            *two(NY),
            *two(2, NZ // 2 + 1),
            *two(2, NX),
            *two(3, NY),
            *two(3, NY),
            *two(2, NY // 2 + 1, 2),
            *two(2, NY // 2 + 1),
            *two(2, NX),
            *two(2, NZ // 2 + 1, 2),
            *two(NY),
        ],
        compiler_params=pltpu.CompilerParams(
            collective_id=0, has_side_effects=True, vmem_limit_bytes=52 << 20
        ),
        name="layer",
    )(*operands)


def on_device(
    queries,
    latent_cache,
    ancestors,
    value_up,
    out_proj,
    residual,
    norm_gain,
    routes,
    gates,
    w_gate,
    w_up,
    w_down,
):
    final = layer(
        ancestors,
        ancestors,
        queries.transpose(1, 0, 2),
        value_up,
        routes,
        gates,
        residual,
        norm_gain.astype(F32).reshape(NY, 1, DY),
        latent_cache,
        out_proj,
        w_gate[0],
        w_up[0],
        w_down[0],
    )
    return final.astype(BF16)


def solution(mesh):
    placed = (
        P("seq", "exp", None),
        P("seq", None, None),
        P("seq", None),
        P("exp", None, None),
        P("exp", None),
        P(("seq", "exp"), None),
        P(),
        P(("seq", "exp"), None),
        P(("seq", "exp"), None),
        P("exp", None, "seq"),
        P("exp", None, "seq"),
        P("exp", "seq", None),
    )
    return jax.shard_map(
        on_device, mesh=mesh, in_specs=placed, out_specs=P(("seq", "exp"), None), check_vma=False
    )
```

time: 730 us -> 200 us (0.27)
  waiting for transfers between devices: 519 us -> 0 us
  Pallas kernels: 0 us -> 192 us
  local copies, waits for them, and re-layouts: 96 us -> 6.23 us
  blocking collectives: 47.7 us -> 0 us
  matrix products: 31.8 us -> 0 us
  between operations: 14 us -> 0.03 us
  starting transfers between devices: 10.5 us -> 0 us
    reduce_scatter x1 -> x0, waiting for transfers between devices: 219 us -> none  [on_device(): lax.psum_scatter(jnp.dot(rows, out_proj, preferred_element_type=jnp.float...]
    pallas_call x0 -> x1, Pallas kernels: none -> 192 us  [layer(): pl.pallas_call(layer_kernel, out_shape=jax.ShapeDtypeStruct((8, D), F32),...]
    unnamed x5 -> x0, waiting for transfers between devices: 168 us -> none
    all_gather x2 -> x0, waiting for transfers between devices: 90.6 us -> none  [the longest x1 60.5 us: on_device(): piece = lax.all_gather(arrived, 'seq', axis=0, tiled=True)]
    all_to_all x1 -> x0, blocking collectives: 47.7 us -> none  [on_device(): lax.all_to_all(buffer, 'exp', split_axis=0, concat_axis=0, tiled=True)]
    all_to_all x1 -> x0, waiting for transfers between devices: 40.8 us -> none  [on_device(): lax.all_to_all(summed_rows, 'exp', split_axis=0, concat_axis=0, tiled=True)]
    dot_general x7 -> x0, matrix products: 31.8 us -> none  [the longest x1 17.3 us: on_device(): jnp.dot(act, down_local, preferred_element_type=jnp.float32)]
    reshape x3 -> x0, local copies, waits for them, and re-layouts: 28.4 us -> none  [the longest x1 24.9 us: on_device(): rows = piece.reshape(-1, D)]
  transfers between devices with their start and end apart: 5 -> 0, of which waited for: 5 -> 0; matrix products, arithmetic and copies ran while one was open for 1% -> 0% of each run, Pallas kernels for 0% -> 0%
where the time goes in v2:
time: 200 us
  Pallas kernels  192 us (96%)
  local copies, waits for them, and re-layouts  6.23 us (3%)
    pallas_call x1, Pallas kernels, layer(): pl.pallas_call(layer_kernel, out_shape=jax.ShapeDtypeStruct((8, D), F32),...  192 us
    unnamed x13, local copies, waits for them, and re-layouts  6.23 us

profile of v2, /device:TPU:32, one launch (start us, length us, event | category | flops | bytes accessed | tf_op | source)
XLA Modules:
  0.0 199.5 jit_solution(12982715316614626215)
XLA Ops:
  0.0 0.7 reshape.7
  0.7 1.4 copy.13
  2.1 0.0 copy-start
  2.1 1.0 copy-done
  3.1 0.0 copy-start.1
  3.1 0.9 copy-done.1
  4.0 0.0 copy-start.2
  4.0 0.9 copy-done.2
  4.9 0.0 copy-start.3
  4.9 0.7 copy-done.3
  5.6 0.0 copy-start.4
  5.6 0.7 copy-done.4
  6.3 0.0 copy-start.5
  6.3 0.7 copy-done.5
  7.0 191.9 %layer.1 = f32[8,7168]{1,0:T(8,128)S(1)} custom-call(s32[4,8]{1,0:T(4,128)S(1)} %copy-done.3, s32[4,8]{1,0:T(4,128)S(1)} %copy-done.3, bf16[2,256,576]{2,1,0:T(8,128)(2,1)S(1)} %bitcast.5, bf16[2,512,128]{2,1,0:T(8,128)(2,1)S(1)} %copy-done.1, s32[8,8]{1,0:T(8,128)S(1)} %copy-done.4, f32[8,8]{1,0:T(8,128)S(1)} %copy-done.5, bf16[8,7168]{1,0:T(8,128)(2,1)S(1)} %copy-done.2, ...), custom_call_target="tpu_custom_call" | custom-call | tf_op jit(solution)/shard_map/layer/pallas_call | solution.py:533
  198.8 0.7 convert_element_type.4
Async XLA Ops:
  2.1 1.0 copy-start
  3.1 0.9 copy-start.1
  4.0 0.9 copy-start.2
  4.9 0.7 copy-start.3
  5.6 0.7 copy-start.4
  6.3 0.7 copy-start.5

commit v3 on v2

--- a/solution.py
+++ b/solution.py
@@ -83,26 +83,34 @@
 
 def ring_gather(links, axis, count, me, view, half, send_sem, recv_sem):
     last = count // 2
+
+    def got(way, step, part):
+        links.arrived(
+            half(view(-(1, -1)[way] * step, 0), part),
+            send_sem.at[way, step, part],
+            recv_sem.at[way, step, part],
+        )
+
     for step in range(1, last + 1):
         new = []
-        for way, sign in enumerate((1, -1)):
-            k = -sign * (step - 1)
-            if step > 1:
-                links.arrived(view(k, 0), send_sem.at[way, step - 1], recv_sem.at[way, step - 1])
-                new.append(k)
-            src, dst = view(k, 0), view(k, sign)
-            if step == last:
-                src, dst = half(src, way), half(dst, way)
-            links.send(
-                src, dst, send_sem.at[way, step], recv_sem.at[way, step],
-                **{axis: wrap(me + sign, count)},
-            )
+        for part_at in range(2):
+            for way, sign in enumerate((1, -1)):
+                part = way if part_at == 0 else 1 - way
+                k = -sign * (step - 1)
+                if step > 1:
+                    got(way, step - 1, part)
+                    if part_at:
+                        new.append(k)
+                if step < last or part == way:
+                    links.send(
+                        half(view(k, 0), part), half(view(k, sign), part),
+                        send_sem.at[way, step, part], recv_sem.at[way, step, part],
+                        **{axis: wrap(me + sign, count)},
+                    )
         if new:
             yield new
-    for way, sign in enumerate((1, -1)):
-        links.arrived(
-            half(view(-sign * last, 0), way), send_sem.at[way, last], recv_sem.at[way, last]
-        )
+    for way in range(2):
+        got(way, last, way)
     yield [last]
 
 
@@ -110,8 +118,9 @@
     last = count // 2
     for step in range(1, last + 1):
         yield step
-        for h in range(2):
+        for part_at in range(2):
             for way, sign in enumerate((1, -1)):
+                h = 1 - way if part_at == 0 else way
                 if step == 1 and h != way:
                     continue
                 value = own(sign * (last + 1 - step), h)
@@ -201,8 +210,9 @@
 
 
 def layer_kernel(
-    anc, anc_rows, q, vup, routes, gates, res, gain, lat_in, outp, wg, wu, wd,
+    anc, q_in, vup_in, gates_in, res_in, routes_in, anc_in, gain_in, lat_in, outp, wg, wu, wd,
     out,
+    q, vup, gates, res, routes, anc_rows, gain,
     lat, keys, meta, meta_all, res32, res_y, op_all, ho_a, ho_b, partial, a_sent, a_got,
     att, xrecv, hidden, squares, tokens, choose, combine, disp, rows, w_in, w_out,
     gsend, g_sent, g_got, act, dout, back, comb, c_sent, c_got, fin, orecv,
@@ -226,6 +236,21 @@
             return w_out.at[pl.ds(pl.multiple_of(src * 128, 128), 128), :]
         return w_in.at[:, pl.ds(pl.multiple_of(k * FF + src * 128, 128), 128)]
 
+    def send_weights(k, d):
+        to = wrap(y + d, NY)
+        send(weight_source(k, to), weight_place(k, s), w_s.at[k, d], w_r.at[k, d], y=to)
+
+    def pass_on(k, d):
+        block = weight_place(k, wrap(y - d, NY) * 2 + c)
+        arrived(block, w_s.at[k, d], w_r.at[k, d])
+        send(block, block, f_s.at[k, d], f_r.at[k, d], c=other)
+
+    def from_other(k):
+        own[2 + k].wait()
+        for d in range(NY):
+            block = weight_place(k, wrap(y - d, NY) * 2 + other)
+            arrived(block, f_s.at[k, d], f_r.at[k, d])
+
     def op_columns(to):
         start = pl.multiple_of(y * DY + jnp.minimum(to * CW, DY - CW), 128)
         return outp.at[:, pl.ds(start, CW)]
@@ -237,8 +262,24 @@
         pltpu.make_async_copy(weight_source(k, y), weight_place(k, s), loc.at[2 + k])
         for k in range(3)
     ]
-    for copy in own:
+    small = [
+        pltpu.make_async_copy(src, dst, loc.at[5 + k])
+        for k, (src, dst) in enumerate(
+            (
+                (routes_in, routes),
+                (gates_in, gates),
+                (res_in, res),
+                (anc_in, anc_rows),
+                (gain_in, gain),
+                (q_in, q),
+                (vup_in, vup),
+            )
+        )
+    ]
+    for copy in own[:1] + small + own[1:]:
         copy.start()
+    for copy in small[:3]:
+        copy.wait()
     meta[...] = routing_table(routes[...], gates[...])
     meta_all[1, y] = meta[...]
     res32[...] = res[...].astype(F32)
@@ -269,10 +310,9 @@
     forward(0)
     for k in first:
         forward(k)
-    for d in range(1, NY):
-        to = wrap(y + d, NY)
-        part = res32.at[:, pl.ds(pl.multiple_of(to * DY, 128), DY)]
-        send(part, res_y.at[y], re_s.at[d], re_r.at[d], y=to)
+    for k in range(2):
+        for d in (1, 3):
+            send_weights(k, d)
     for d in range(1, NX):
         to = wrap(x + d, NX)
         send(op_columns(to), op_all.at[x], op_s.at[d], op_r.at[d], x=to)
@@ -281,6 +321,8 @@
     for d in range(1, NZ):
         send(meta_all.at[1], meta_all.at[(d + 1) % NZ], mz_s.at[d], mz_r.at[d], z=wrap(z + d, NZ))
     res_y[y] = res32[:, pl.ds(pl.multiple_of(y * DY, 128), DY)]
+    for copy in small[3:]:
+        copy.wait()
     area = lax.broadcasted_iota(jnp.int32, (ANC, (ANC + 1) * BLK), 1)
     slot_of = lax.broadcasted_iota(jnp.int32, (ANC, (ANC + 1) * BLK), 0)
     spread = (lax.div(area, BLK) == slot_of).astype(F32)
@@ -294,9 +336,6 @@
         send(
             weight_source(k, y), weight_place(k, s), f_s.at[k, 0], f_r.at[k, 0], c=other
         )
-    for d in (1, 3):
-        to = wrap(y + d, NY)
-        send(weight_source(2, to), weight_place(2, s), w_s.at[2, d], w_r.at[2, d], y=to)
     for k in range(NY):
         block = lat.at[pl.ds((wrap(y + k, NY) * 2 + other) * 4, 4)]
         arrived(block, fwd_s.at[k], fwd_r.at[k])
@@ -336,10 +375,15 @@
     own[1].wait()
     drain(a_ring)
     drain(b_ring)
+    for d in range(1, NY):
+        to = wrap(y + d, NY)
+        part = res32.at[:, pl.ds(pl.multiple_of(to * DY, 128), DY)]
+        send(part, res_y.at[y], re_s.at[d], re_r.at[d], y=to)
+    send_weights(0, 2)
+    send_weights(1, 2)
     for k in range(2):
         for d in (1, 3):
-            to = wrap(y + d, NY)
-            send(weight_source(k, to), weight_place(k, s), w_s.at[k, d], w_r.at[k, d], y=to)
+            pass_on(k, d)
 
     for n in range(NY):
         for low, block in ((0, lambda k: ho_a[n, k]), (4, lambda k: ho_b[k, n])):
@@ -367,9 +411,6 @@
         to = wrap(x + d, NX)
         send(att.at[to], xrecv.at[x], xa_s.at[d], xa_r.at[d], x=to)
     xrecv[x] = att[x]
-    to = wrap(y + 2, NY)
-    for k in range(3):
-        send(weight_source(k, to), weight_place(k, s), w_s.at[k, 2], w_r.at[k, 2], y=to)
     for d in range(1, NY):
         arrived(res_y.at[wrap(y - d, NY)], re_s.at[d], re_r.at[d])
     for d in range(1, NX):
@@ -386,6 +427,8 @@
         send(squares.at[y], squares.at[y], sq_s.at[d], sq_r.at[d], y=wrap(y + d, NY))
     for d in range(1, NY):
         arrived(squares.at[wrap(y - d, NY)], sq_s.at[d], sq_r.at[d])
+    for d in (1, 3, 2):
+        send_weights(2, d)
     mean = (squares[0] + squares[1] + squares[2] + squares[3])[:, :1] * (1.0 / D)
     tokens[1] = (held * lax.rsqrt(mean + NORM_EPS) * gain[y]).astype(BF16)
     token_ring = ring_gather(
@@ -407,28 +450,14 @@
             send(disp.at[h, to], rows.at[x, h], dp_s.at[h, d], dp_r.at[h, d], x=to)
         rows[x, h] = disp[h, x]
 
-    def pass_on(k, d):
-        block = weight_place(k, wrap(y - d, NY) * 2 + c)
-        arrived(block, w_s.at[k, d], w_r.at[k, d])
-        send(block, block, f_s.at[k, d], f_r.at[k, d], c=other)
-
-    def from_other(k):
-        own[2 + k].wait()
-        for d in range(NY):
-            block = weight_place(k, wrap(y - d, NY) * 2 + other)
-            arrived(block, f_s.at[k, d], f_r.at[k, d])
-
     next(token_ring)
     next(token_ring)
     dispatch(0)
     next(token_ring)
-    for k in (2, 0, 1):
-        for d in (1, 3):
-            pass_on(k, d)
+    for k in range(2):
+        pass_on(k, 2)
     drain(token_ring)
     dispatch(1)
-    for k in range(2):
-        pass_on(k, 2)
     for k in range(2):
         from_other(k)
 
@@ -464,7 +493,8 @@
         ac_s, ac_r,
     )
     next(act_ring)
-    pass_on(2, 2)
+    for d in (1, 3, 2):
+        pass_on(2, d)
     from_other(2)
     drain(act_ring)
 
@@ -533,9 +563,16 @@
     return pl.pallas_call(
         layer_kernel,
         out_shape=jax.ShapeDtypeStruct((8, D), F32),
-        in_specs=[SMEM] + [VMEM] * 7 + [ANY] * 5,
+        in_specs=[SMEM] + [ANY] * 12,
         out_specs=VMEM,
         scratch_shapes=[
+            pltpu.VMEM((2, 256, LAT + ROPE), BF16),
+            pltpu.VMEM((2, LAT, HD), BF16),
+            pltpu.VMEM((8, TOP), F32),
+            pltpu.VMEM((8, D), BF16),
+            pltpu.VMEM((8, TOP), jnp.int32),
+            pltpu.VMEM((4, ANC), jnp.int32),
+            pltpu.VMEM((NY, 1, DY), F32),
             pltpu.VMEM((32, BLK, LAT + ROPE), BF16),
             pltpu.VMEM(((ANC + 1) * BLK, LAT + ROPE), BF16),
             pltpu.VMEM((8, 128), F32),
@@ -570,8 +607,8 @@
             pltpu.VMEM((2, NZ // 2 + 1, 2, 16, DY), BF16),
             pltpu.VMEM((NY, 8, DY), F32),
             pltpu.VMEM((NY, 8, DY), F32),
-            DMA((5,)),
-            *two(2, NY // 2 + 1),
+            DMA((12,)),
+            *two(2, NY // 2 + 1, 2),
             *two(NY),
             *two(NX),
             *two(NY),
@@ -579,23 +616,23 @@
             *two(NY),
             *two(NX),
             *two(NY),
-            *two(2, NY // 2 + 1),
-            *two(2, NX // 2 + 1),
+            *two(2, NY // 2 + 1, 2),
+            *two(2, NX // 2 + 1, 2),
             *two(2, NZ // 2 + 1, 2),
             *two(NX),
             *two(NY),
-            *two(2, NZ // 2 + 1),
+            *two(2, NZ // 2 + 1, 2),
             *two(2, NX),
             *two(3, NY),
             *two(3, NY),
             *two(2, NY // 2 + 1, 2),
-            *two(2, NY // 2 + 1),
+            *two(2, NY // 2 + 1, 2),
             *two(2, NX),
             *two(2, NZ // 2 + 1, 2),
             *two(NY),
         ],
         compiler_params=pltpu.CompilerParams(
-            collective_id=0, has_side_effects=True, vmem_limit_bytes=52 << 20
+            collective_id=0, has_side_effects=True, vmem_limit_bytes=63 << 20
         ),
         name="layer",
     )(*operands)
@@ -617,12 +654,12 @@
 ):
     final = layer(
         ancestors,
-        ancestors,
         queries.transpose(1, 0, 2),
         value_up,
-        routes,
         gates,
         residual,
+        routes,
+        ancestors,
         norm_gain.astype(F32).reshape(NY, 1, DY),
         latent_cache,
         out_proj,

time: 200 us -> 177 us (0.89)
  Pallas kernels: 192 us -> 172 us
  local copies, waits for them, and re-layouts: 6.23 us -> 2.14 us
    pallas_call x1, Pallas kernels: 192 us -> 172 us  [layer(): pl.pallas_call(layer_kernel, out_shape=jax.ShapeDtypeStruct((8, D), F32),...]
    unnamed x13 -> x1, local copies, waits for them, and re-layouts: 6.23 us -> 2.14 us
where the time goes in v3:
time: 177 us
  Pallas kernels  172 us (97%)
  other arithmetic  2.92 us (2%)
  local copies, waits for them, and re-layouts  2.14 us (1%)
    pallas_call x1, Pallas kernels, layer(): pl.pallas_call(layer_kernel, out_shape=jax.ShapeDtypeStruct((8, D), F32),...  172 us

profile of v3, /device:TPU:32, one launch (start us, length us, event | category | flops | bytes accessed | tf_op | source)
XLA Modules:
  0.0 176.6 jit_solution(4769638975732202668)
XLA Ops:
  0.0 1.3 reshape.7
  1.3 2.1 %copy.13 = bf16[256,2,576]{2,0,1:T(8,128)(2,1)} copy(bf16[256,2,576]{0,2,1:T(8,128)(2,1)} %param.12) | data formatting | bytes 1179648 | tf_op args[0]
  3.5 171.5 %layer.1 = f32[8,7168]{1,0:T(8,128)} custom-call(s32[4,8]{1,0:T(4,128)} %anc_in.1, bf16[2,256,576]{2,1,0:T(8,128)(2,1)} %bitcast.5, bf16[2,512,128]{2,1,0:T(8,128)(2,1)} %vup_in.1, f32[8,8]{1,0:T(8,128)} %gates_in.1, bf16[8,7168]{1,0:T(8,128)(2,1)} %res_in.1, s32[8,8]{1,0:T(8,128)} %routes_in.1, s32[4,8]{1,0:T(4,128)} %anc_in.1, f32[4,1,1792]{2,1,0:T(1,128)} %bitcast.9, ...), custom_call_target="tpu_custom_call" | custom-call | tf_op jit(solution)/shard_map/layer/pallas_call | solution.py:563
  175.0 1.6 convert_element_type.4

commit v4 on v3

--- a/solution.py
+++ b/solution.py
@@ -137,6 +137,7 @@
                     send_sem.at[way, step, h], recv_sem.at[way, step, h],
                     **{axis: wrap(me + sign, count)},
                 )
+    yield last + 1
     for h in range(2):
         for way in range(2):
             links.arrived(
@@ -212,7 +213,7 @@
 def layer_kernel(
     anc, q_in, vup_in, gates_in, res_in, routes_in, anc_in, gain_in, lat_in, outp, wg, wu, wd,
     out,
-    q, vup, gates, res, routes, anc_rows, gain,
+    q, q_turned, vup, gates, res, routes, anc_rows, gain,
     lat, keys, meta, meta_all, res32, res_y, op_all, ho_a, ho_b, partial, a_sent, a_got,
     att, xrecv, hidden, squares, tokens, choose, combine, disp, rows, w_in, w_out,
     gsend, g_sent, g_got, act, dout, back, comb, c_sent, c_got, fin, orecv,
@@ -271,7 +272,7 @@
                 (res_in, res),
                 (anc_in, anc_rows),
                 (gain_in, gain),
-                (q_in, q),
+                (q_in, q_turned),
                 (vup_in, vup),
             )
         )
@@ -323,6 +324,8 @@
     res_y[y] = res32[:, pl.ds(pl.multiple_of(y * DY, 128), DY)]
     for copy in small[3:]:
         copy.wait()
+    for h in range(2):
+        q[h] = q_turned[h].T
     area = lax.broadcasted_iota(jnp.int32, (ANC, (ANC + 1) * BLK), 1)
     slot_of = lax.broadcasted_iota(jnp.int32, (ANC, (ANC + 1) * BLK), 0)
     spread = (lax.div(area, BLK) == slot_of).astype(F32)
@@ -430,7 +433,7 @@
     for d in (1, 3, 2):
         send_weights(2, d)
     mean = (squares[0] + squares[1] + squares[2] + squares[3])[:, :1] * (1.0 / D)
-    tokens[1] = (held * lax.rsqrt(mean + NORM_EPS) * gain[y]).astype(BF16)
+    tokens[1] = (held * lax.rsqrt(mean + NORM_EPS) * gain[pl.ds(pl.multiple_of(y * DY, 256), DY)].astype(F32).reshape(1, DY)).astype(BF16)
     token_ring = ring_gather(
         links, "z", NZ, z,
         lambda k, shift: tokens.at[(1 - k + shift) % NZ],
@@ -460,8 +463,10 @@
     dispatch(1)
     for k in range(2):
         from_other(k)
-
-    for h in range(2):
+    for d in (1, 3, 2):
+        pass_on(2, d)
+
+    def enter(h):
         for d in range(1, NX):
             arrived(rows.at[wrap(x - d, NX), h], dp_s.at[h, d], dp_r.at[h, d])
 
@@ -476,29 +481,33 @@
 
         lax.fori_loop(0, 2 * FF // 512, inward, 0)
 
-    def inward_term(k, h):
-        return gsend[wrap(y + k, NY), h].astype(F32)
-
-    drain(ring_reduce(links, "y", NY, y, inward_term, g_sent, g_got, gy_s, gy_r))
-    for h in range(2):
-        total = (
-            inward_term(0, h)
-            + g_got[0, NY // 2, h].astype(F32)
-            + g_got[1, NY // 2, h].astype(F32)
-        )
-        gate = total[:, :FF]
-        act[y, h] = (gate / (1.0 + jnp.exp(-gate)) * total[:, FF:]).astype(BF16)
-    act_ring = ring_gather(
-        links, "y", NY, y, lambda k, shift: act.at[wrap(y + k, NY)], lambda ref, h: ref.at[h],
-        ac_s, ac_r,
-    )
-    next(act_ring)
-    for d in (1, 3, 2):
-        pass_on(2, d)
-    from_other(2)
-    drain(act_ring)
-
-    for h in (1, 0):
+    def inward_term(h):
+        return lambda k, part: gsend[
+            wrap(y + k, NY), h, :, part * FF : (part + 1) * FF
+        ].astype(F32)
+
+    def sum_ring(h):
+        return ring_reduce(
+            links, "y", NY, y, inward_term(h), g_sent.at[h], g_got.at[h], gy_s.at[h], gy_r.at[h]
+        )
+
+    def activate(h):
+        gate, up = (
+            inward_term(h)(0, part)
+            + g_got[h, 0, NY // 2, part].astype(F32)
+            + g_got[h, 1, NY // 2, part].astype(F32)
+            for part in range(2)
+        )
+        act[y, h] = (gate / (1.0 + jnp.exp(-gate)) * up).astype(BF16)
+
+    def act_ring(h):
+        return ring_gather(
+            links, "y", NY, y, lambda k, shift: act.at[wrap(y + k, NY), h],
+            lambda ref, part: ref.at[:, pl.ds(part * (FF // 2), FF // 2)],
+            ac_s.at[h], ac_r.at[h],
+        )
+
+    def leave(h):
         def outward(j, _):
             at = pl.ds(pl.multiple_of(j * 256, 256), 256)
             part = jnp.dot(
@@ -514,6 +523,28 @@
             send(dout.at[h, to], back.at[h, x], bk_s.at[h, d], bk_r.at[h, d], x=to)
         back[h, x] = dout[h, x]
 
+    sums = [sum_ring(0), sum_ring(1)]
+    acts = [act_ring(0), act_ring(1)]
+    enter(0)
+    for _ in range(3):
+        next(sums[0])
+    enter(1)
+    next(sums[1])
+    next(sums[1])
+    drain(sums[0])
+    activate(0)
+    next(acts[0])
+    next(acts[0])
+    next(sums[1])
+    drain(acts[0])
+    from_other(2)
+    drain(sums[1])
+    activate(1)
+    next(acts[1])
+    leave(0)
+    drain(acts[1])
+    leave(1)
+
     def weigh_rows(h):
         for d in range(1, NX):
             arrived(back.at[h, wrap(x - d, NX)], bk_s.at[h, d], bk_r.at[h, d])
@@ -532,10 +563,9 @@
     def token_term(k, h):
         return comb[(1 - k) % NZ, h * 16 : (h + 1) * 16]
 
+    weigh_rows(0)
     weigh_rows(1)
-    for step in ring_reduce(links, "z", NZ, z, token_term, c_sent, c_got, zc_s, zc_r):
-        if step == 3:
-            weigh_rows(0)
+    drain(ring_reduce(links, "z", NZ, z, token_term, c_sent, c_got, zc_s, zc_r))
     for h in range(2):
         total = (
             hidden[h * 16 : (h + 1) * 16]
@@ -567,12 +597,13 @@
         out_specs=VMEM,
         scratch_shapes=[
             pltpu.VMEM((2, 256, LAT + ROPE), BF16),
+            pltpu.VMEM((2, LAT + ROPE, 256), BF16),
             pltpu.VMEM((2, LAT, HD), BF16),
             pltpu.VMEM((8, TOP), F32),
             pltpu.VMEM((8, D), BF16),
             pltpu.VMEM((8, TOP), jnp.int32),
             pltpu.VMEM((4, ANC), jnp.int32),
-            pltpu.VMEM((NY, 1, DY), F32),
+            pltpu.VMEM((D,), BF16),
             pltpu.VMEM((32, BLK, LAT + ROPE), BF16),
             pltpu.VMEM(((ANC + 1) * BLK, LAT + ROPE), BF16),
             pltpu.VMEM((8, 128), F32),
@@ -597,8 +628,8 @@
             pltpu.VMEM((DY, 2 * FF), BF16),
             pltpu.VMEM((FF, DY), BF16),
             pltpu.VMEM((NY, 2, HALF, 2 * FF), BF16),
-            pltpu.VMEM((2, NY // 2 + 1, 2, HALF, 2 * FF), BF16),
-            pltpu.VMEM((2, NY // 2 + 1, 2, HALF, 2 * FF), BF16),
+            pltpu.VMEM((2, 2, NY // 2 + 1, 2, HALF, FF), BF16),
+            pltpu.VMEM((2, 2, NY // 2 + 1, 2, HALF, FF), BF16),
             pltpu.VMEM((NY, 2, HALF, FF), BF16),
             pltpu.VMEM((2, NX, HALF, DY), BF16),
             pltpu.VMEM((2, NX, HALF, DY), BF16),
@@ -625,8 +656,8 @@
             *two(2, NX),
             *two(3, NY),
             *two(3, NY),
-            *two(2, NY // 2 + 1, 2),
-            *two(2, NY // 2 + 1, 2),
+            *two(2, 2, NY // 2 + 1, 2),
+            *two(2, 2, NY // 2 + 1, 2),
             *two(2, NX),
             *two(2, NZ // 2 + 1, 2),
             *two(NY),
@@ -654,13 +685,13 @@
 ):
     final = layer(
         ancestors,
-        queries.transpose(1, 0, 2),
+        queries.transpose(1, 2, 0),
         value_up,
         gates,
         residual,
         routes,
         ancestors,
-        norm_gain.astype(F32).reshape(NY, 1, DY),
+        norm_gain,
         latent_cache,
         out_proj,
         w_gate[0],

time: 177 us -> 175 us (0.989)
  local copies, waits for them, and re-layouts: 2.14 us -> 0 us
    unnamed x1 -> x0, local copies, waits for them, and re-layouts: 2.14 us -> none
where the time goes in v4:
time: 175 us; the launch traced here: 174 us
  Pallas kernels  172 us (98%)
    pallas_call x1, Pallas kernels, layer(): pl.pallas_call(layer_kernel, out_shape=jax.ShapeDtypeStruct((8, D), F32),...  172 us

profile of v4, /device:TPU:32, one launch (start us, length us, event | category | flops | bytes accessed | tf_op | source)
XLA Modules:
  0.0 173.5 jit_solution(3413846860396891082)
XLA Ops:
  0.0 171.9 %layer.1 = f32[8,7168]{1,0:T(8,128)} custom-call(s32[4,8]{1,0:T(4,128)} %anc_in.1, bf16[2,576,256]{2,1,0:T(8,128)(2,1)} %bitcast.7, bf16[2,512,128]{2,1,0:T(8,128)(2,1)} %vup_in.1, f32[8,8]{1,0:T(8,128)} %gates_in.1, bf16[8,7168]{1,0:T(8,128)(2,1)} %res_in.1, s32[8,8]{1,0:T(8,128)} %routes_in.1, s32[4,8]{1,0:T(4,128)} %anc_in.1, bf16[7168]{0:T(1024)(128)(2,1)} %gain_in.1, ...), custom_call_target="tpu_custom_call" | custom-call | tf_op jit(solution)/shard_map/layer/pallas_call | solution.py:593
  171.9 1.6 convert_element_type.3

commit v5 on v4

--- a/solution.py
+++ b/solution.py
@@ -371,7 +371,7 @@
         arrived(meta_all.at[(d + 1) % NZ], mz_s.at[d], mz_r.at[d])
     for h in range(2):
         pick, weigh = matches(meta_all[4 * h : 4 * h + 4].reshape(128, 128), z)
-        choose[h] = pick
+        choose[h] = pick.T
         combine[h] = weigh
     for d in range(1, NX):
         arrived(op_all.at[wrap(x - d, NX)], op_s.at[d], op_r.at[d])
@@ -402,14 +402,17 @@
         return partial[wrap(z + k, NZ), 2 * h : 2 * h + 2].astype(F32)
 
     drain(ring_reduce(links, "z", NZ, z, attention_term, a_sent, a_got, za_s, za_r))
-    for h in range(2):
-        total = (
+    summed = jnp.concatenate(
+        [
             attention_term(0, h)
             + a_got[0, NZ // 2, h].astype(F32)
             + a_got[1, NZ // 2, h].astype(F32)
-        )
-        for k in range(NX):
-            att[k, 2 * h : 2 * h + 2] = total[:, k * 8 : (k + 1) * 8]
+            for h in range(2)
+        ],
+        axis=0,
+    )
+    for k in range(NX):
+        att[k] = summed[:, k * 8 : (k + 1) * 8].reshape(NY * 8, CW).astype(BF16)
     for d in range(1, NX):
         to = wrap(x + d, NX)
         send(att.at[to], xrecv.at[x], xa_s.at[d], xa_r.at[d], x=to)
@@ -421,7 +424,7 @@
     for k in range(NX):
         low = NX * CW - DY if k == NX - 1 else 0
         at, wide = k * CW, CW - low
-        hidden[:, at : at + wide] = xrecv[k].reshape(NY * 8, CW)[:, low:] + res_y[
+        hidden[:, at : at + wide] = xrecv[k, :, low:].astype(F32) + res_y[
             :, :, at : at + wide
         ].reshape(NY * 8, wide)
     held = hidden[...]
@@ -443,9 +446,7 @@
 
     def dispatch(h):
         table = tokens[4 * h : 4 * h + 4].reshape(128, DY)
-        chosen = lax.dot_general(
-            choose[h], table, (((0,), (0,)), ((), ())), preferred_element_type=F32
-        ).astype(BF16)
+        chosen = jnp.dot(choose[h], table, preferred_element_type=F32).astype(BF16)
         for k in range(NX):
             disp[h, k] = chosen[k * HALF : (k + 1) * HALF]
         for d in (2, 1, 3):
@@ -463,8 +464,6 @@
     dispatch(1)
     for k in range(2):
         from_other(k)
-    for d in (1, 3, 2):
-        pass_on(2, d)
 
     def enter(h):
         for d in range(1, NX):
@@ -537,10 +536,12 @@
     next(acts[0])
     next(sums[1])
     drain(acts[0])
-    from_other(2)
+    for d in (1, 3, 2):
+        pass_on(2, d)
     drain(sums[1])
     activate(1)
     next(acts[1])
+    from_other(2)
     leave(0)
     drain(acts[1])
     leave(1)
@@ -573,8 +574,11 @@
             + c_got[0, NZ // 2, h].astype(F32)
             + c_got[1, NZ // 2, h].astype(F32)
         )
-        fin[2 * h] = total[:8]
-        fin[2 * h + 1] = total[8:]
+        for k in range(2):
+            block = total[k * 8 : (k + 1) * 8]
+            fin[2 * h + k] = jnp.concatenate(
+                [block[:, : DY // 2], block[:, DY // 2 :]], axis=0
+            ).astype(BF16)
     for d in (2, 1, 3):
         to = wrap(y + d, NY)
         send(fin.at[to], orecv.at[y], fo_s.at[d], fo_r.at[d], y=to)
@@ -582,7 +586,9 @@
     for d in range(1, NY):
         arrived(orecv.at[wrap(y - d, NY)], fo_s.at[d], fo_r.at[d])
     for k in range(NY):
-        out[:, k * DY : (k + 1) * DY] = orecv[k]
+        block = orecv[k].astype(F32)
+        out[:, k * DY : k * DY + DY // 2] = block[:8]
+        out[:, k * DY + DY // 2 : (k + 1) * DY] = block[8:]
     links.finish()
 
 
@@ -616,12 +622,12 @@
             pltpu.VMEM((NZ, NY, 32, CW), BF16),
             pltpu.VMEM((2, NZ // 2 + 1, 2, 2, 32, CW), BF16),
             pltpu.VMEM((2, NZ // 2 + 1, 2, 2, 32, CW), BF16),
-            pltpu.VMEM((NX, NY, 8, CW), F32),
-            pltpu.VMEM((NX, NY, 8, CW), F32),
+            pltpu.VMEM((NX, NY * 8, CW), BF16),
+            pltpu.VMEM((NX, NY * 8, CW), BF16),
             pltpu.VMEM((NY * 8, DY), F32),
             pltpu.VMEM((NY, NY * 8, 128), F32),
             pltpu.VMEM((NZ, NY * 8, DY), BF16),
-            pltpu.VMEM((2, 128, NX * HALF), BF16),
+            pltpu.VMEM((2, NX * HALF, 128), BF16),
             pltpu.VMEM((2, 128, NX * HALF), BF16),
             pltpu.VMEM((2, NX, HALF, DY), BF16),
             pltpu.VMEM((NX, 2, HALF, DY), BF16),
@@ -636,8 +642,8 @@
             pltpu.VMEM((NZ, NY * 8, DY), F32),
             pltpu.VMEM((2, NZ // 2 + 1, 2, 16, DY), BF16),
             pltpu.VMEM((2, NZ // 2 + 1, 2, 16, DY), BF16),
-            pltpu.VMEM((NY, 8, DY), F32),
-            pltpu.VMEM((NY, 8, DY), F32),
+            pltpu.VMEM((NY, 16, DY // 2), BF16),
+            pltpu.VMEM((NY, 16, DY // 2), BF16),
             DMA((12,)),
             *two(2, NY // 2 + 1, 2),
             *two(NY),

time: 175 us -> 173 us (0.989)
  no operation moved by 1% of the time
where the time goes in v5:
time: 173 us
  Pallas kernels  171 us (99%)
    pallas_call x1, Pallas kernels, layer(): pl.pallas_call(layer_kernel, out_shape=jax.ShapeDtypeStruct((8, D), F32),...  171 us

profile of v5, /device:TPU:32, one launch (start us, length us, event | category | flops | bytes accessed | tf_op | source)
XLA Modules:
  0.0 172.5 jit_solution(2924814384123363528)
XLA Ops:
  0.0 170.9 %layer.1 = f32[8,7168]{1,0:T(8,128)} custom-call(s32[4,8]{1,0:T(4,128)} %anc_in.1, bf16[2,576,256]{2,1,0:T(8,128)(2,1)} %bitcast.7, bf16[2,512,128]{2,1,0:T(8,128)(2,1)} %vup_in.1, f32[8,8]{1,0:T(8,128)} %gates_in.1, bf16[8,7168]{1,0:T(8,128)(2,1)} %res_in.1, s32[8,8]{1,0:T(8,128)} %routes_in.1, s32[4,8]{1,0:T(4,128)} %anc_in.1, bf16[7168]{0:T(1024)(128)(2,1)} %gain_in.1, ...), custom_call_target="tpu_custom_call" | custom-call | tf_op jit(solution)/shard_map/layer/pallas_call | solution.py:599
  170.9 1.6 convert_element_type.3

commit v6 on v5

--- a/solution.py
+++ b/solution.py
@@ -433,7 +433,7 @@
         send(squares.at[y], squares.at[y], sq_s.at[d], sq_r.at[d], y=wrap(y + d, NY))
     for d in range(1, NY):
         arrived(squares.at[wrap(y - d, NY)], sq_s.at[d], sq_r.at[d])
-    for d in (1, 3, 2):
+    for d in (1, 3):
         send_weights(2, d)
     mean = (squares[0] + squares[1] + squares[2] + squares[3])[:, :1] * (1.0 / D)
     tokens[1] = (held * lax.rsqrt(mean + NORM_EPS) * gain[pl.ds(pl.multiple_of(y * DY, 256), DY)].astype(F32).reshape(1, DY)).astype(BF16)
@@ -527,6 +527,7 @@
     enter(0)
     for _ in range(3):
         next(sums[0])
+    send_weights(2, 2)
     enter(1)
     next(sums[1])
     next(sums[1])

time: 173 us -> 183 us (1.058)
  Pallas kernels: 171 us -> 181 us
    pallas_call x1, Pallas kernels: 171 us -> 181 us  [layer(): pl.pallas_call(layer_kernel, out_shape=jax.ShapeDtypeStruct((8, D), F32),...]
where the time goes in v6:
time: 183 us
  Pallas kernels  181 us (99%)
    pallas_call x1, Pallas kernels, layer(): pl.pallas_call(layer_kernel, out_shape=jax.ShapeDtypeStruct((8, D), F32),...  181 us

profile of v6, /device:TPU:32, one launch (start us, length us, event | category | flops | bytes accessed | tf_op | source)
XLA Modules:
  0.0 183.0 jit_solution(3723311878528954707)
XLA Ops:
  0.0 181.4 %layer.1 = f32[8,7168]{1,0:T(8,128)} custom-call(s32[4,8]{1,0:T(4,128)} %anc_in.1, bf16[2,576,256]{2,1,0:T(8,128)(2,1)} %bitcast.7, bf16[2,512,128]{2,1,0:T(8,128)(2,1)} %vup_in.1, f32[8,8]{1,0:T(8,128)} %gates_in.1, bf16[8,7168]{1,0:T(8,128)(2,1)} %res_in.1, s32[8,8]{1,0:T(8,128)} %routes_in.1, s32[4,8]{1,0:T(4,128)} %anc_in.1, bf16[7168]{0:T(1024)(128)(2,1)} %gain_in.1, ...), custom_call_target="tpu_custom_call" | custom-call | tf_op jit(solution)/shard_map/layer/pallas_call | solution.py:600
  181.4 1.6 convert_element_type.3
